TPU v7x, 512 devices: a whole 4x8x8 slice. The times are simulated.
512 devices in a mesh: dp: 64 (over x, z, core), tensor: 8 (over y).
Axes of the slice: x: 4, y: 8, z: 8, core: 2. Of those that a mesh axis runs over, the one named last changes fastest.
Arguments:
- token_ids: int32 [2, 128, 64], P(None, 'dp'), may hold values from 0 to 250111
- lengths: int32 [2, 128], P(None, 'dp'), may hold values from 8 to 64, as said below
- positives: int32 [128], P('dp'), may hold values from 0 to 127, each once
- embed_table: bfloat16 [2048, 250112], P('dp', 'tensor'), may hold values from -6 to 6
- norm_gain: float32 [2048], replicated, may hold values from 0.3 to 3
- w_gate: bfloat16 [2048, 3072], P('dp', 'tensor'), may hold values from -0.125 to 0.125
- w_up: bfloat16 [2048, 3072], P('dp', 'tensor'), may hold values from -0.125 to 0.125
- w_down: bfloat16 [3072, 2048], P('tensor', 'dp'), may hold values from -0.109375 to 0.109375
Outputs:
- loss: float32 [], replicated
- grad_up: float32 [2048, 3072], P('dp', 'tensor')
Inputs may be any that keep to these rules, and one draw needn't show every extreme that they name: `lengths`: each query and passage has at least 8 real tokens; some has 64, some has 8. `positives`: every passage is the positive of exactly one query.
All inputs are finite; a program needn't handle non-finite values.
Results may differ from a plain program's by a relative error of at most 0.008.
Values may be sent and summed in bfloat16 or wider, within the bound.
No kernel may reach another device: no remote copies, remote signals or barrier semaphores. Data moves between devices by JAX's collectives and lax.ppermute only.
A program may use at most 64 MiB of HBM per device.

v0:
```python
import jax
import jax.numpy as jnp
from jax import lax
from jax.sharding import PartitionSpec as P

score_scale = 20.0


def rms_scale(values):
    return lax.rsqrt(jnp.mean(values * values, axis=-1, keepdims=True) + 1e-06)


def small_product(left, right, dims):
    return lax.dot_general(left, right, dims, preferred_element_type=jnp.float32)


def on_device(token_ids, lengths, positives, embed_table, norm_gain, w_gate, w_up, w_down):
    dp_count = lax.axis_size("dp")
    pair_dev = token_ids.shape[1]
    seq_len = token_ids.shape[2]
    width = w_down.shape[1] * dp_count
    block_feats = embed_table.shape[0]
    vocab_block = embed_table.shape[1]
    pair_total = pair_dev * dp_count
    all_ids, all_pos = (
        lax.all_gather(token_ids, "dp", axis=1, tiled=True),
        lax.all_gather(positives, "dp", axis=0, tiled=True),
    )
    local_ids = all_ids.reshape(-1) - lax.axis_index("tensor") * vocab_block
    inside = (local_ids >= 0) & (local_ids < vocab_block)
    safe_ids = jnp.clip(local_ids, 0, vocab_block - 1)
    picked = jnp.take(embed_table, safe_ids, axis=1)
    masked = jnp.where(inside[None, :], picked, jnp.zeros((), picked.dtype))
    summed = lax.psum(masked, "tensor").astype(jnp.float32).astype(jnp.bfloat16)
    summed = summed.reshape(block_feats, 2, dp_count, pair_dev * seq_len)
    arrived = lax.all_to_all(summed, "dp", split_axis=2, concat_axis=0, tiled=True)
    embedded = arrived.reshape(width, 2 * pair_dev * seq_len).T
    resid = embedded.astype(jnp.float32)
    normed = (resid * rms_scale(resid) * norm_gain).astype(jnp.bfloat16)
    gate_proj = jnp.dot(
        normed, lax.all_gather(w_gate, "dp", axis=0, tiled=True), preferred_element_type=jnp.float32
    )
    up_proj = jnp.dot(
        normed, lax.all_gather(w_up, "dp", axis=0, tiled=True), preferred_element_type=jnp.float32
    )
    activated = jax.nn.gelu(gate_proj, approximate=True)
    hidden = (activated * up_proj).astype(jnp.bfloat16)
    down_full = lax.all_gather(w_down, "dp", axis=1, tiled=True)
    partial_out = jnp.dot(hidden, down_full, preferred_element_type=jnp.float32)
    states = resid + lax.psum(partial_out, "tensor")
    positions = jnp.arange(seq_len, dtype=jnp.int32)
    pad_mask = (positions[None, None, :] < lengths[:, :, None]).astype(jnp.float32)
    seq_lens = lengths.astype(jnp.float32)
    pooled = (
        jnp.einsum(
            "spt,sptd->spd",
            pad_mask,
            states.reshape(2, pair_dev, seq_len, width),
            precision=lax.Precision.HIGHEST,
        )
        / seq_lens[:, :, None]
    )
    inv_rms = rms_scale(pooled)
    reps = (pooled * inv_rms).astype(jnp.bfloat16)
    factor = score_scale / width
    columns_idx = jnp.arange(pair_total, dtype=jnp.int32)
    contract_last = (((1,), (1,)), ((), ()))
    contract_first = (((0,), (0,)), ((), ()))
    contract_plain = (((1,), (0,)), ((), ()))
    passages = lax.all_gather(reps[1], "dp", axis=0, tiled=True)
    scores = factor * small_product(reps[0], passages, contract_last)
    log_total = jnp.log(jnp.sum(jnp.exp(scores), axis=1))
    one_hot = (columns_idx[None, :] == positives[:, None]).astype(jnp.float32)
    chosen = jnp.sum(scores * one_hot, axis=1)
    ce_total = lax.psum(jnp.sum(log_total - chosen), "dp")
    loss = ce_total / pair_total
    coef = (jnp.exp(scores - log_total[:, None]) - one_hot).astype(jnp.bfloat16)
    grad_query = factor * small_product(coef, passages, contract_plain)
    queries = reps[0]
    grad_passage = lax.psum_scatter(
        factor * small_product(coef, queries, contract_first), "dp", scatter_dimension=0, tiled=True
    )
    grad_reps = jnp.stack([grad_query, grad_passage])
    grad_pooled = (
        inv_rms * grad_reps
        - pooled * inv_rms**3 * jnp.sum(grad_reps * pooled, axis=-1, keepdims=True) / width
    )
    token_grad = (
        ((grad_pooled / seq_lens[:, :, None])[:, :, None, :] * pad_mask[..., None])
        .reshape(-1, width)
        .astype(jnp.bfloat16)
    )
    d_hidden = lax.dot_general(
        token_grad, down_full, contract_last, preferred_element_type=jnp.float32
    )
    d_up = (d_hidden * activated).astype(jnp.bfloat16)
    grad_up = lax.psum_scatter(
        lax.dot_general(normed, d_up, contract_first, preferred_element_type=jnp.float32),
        "dp",
        scatter_dimension=0,
        tiled=True,
    )
    return (loss, grad_up)


def solution(mesh):
    in_specs = (
        P(None, "dp", None),
        P(None, "dp"),
        P("dp"),
        P("dp", "tensor"),
        P(),
        P("dp", "tensor"),
        P("dp", "tensor"),
        P("tensor", "dp"),
    )
    out_specs = (P(), P("dp", "tensor"))
    return jax.shard_map(
        on_device, mesh=mesh, in_specs=in_specs, out_specs=out_specs, check_vma=False
    )
```

profile of v0, /device:TPU:1, one launch (start us, length us, event | category | flops | bytes accessed | tf_op | source)
XLA Modules:
  0.0 902.6 jit_solution(7990238333567703838)
XLA Ops:
  8.7 57.0 %all_gather.15 = s32[2,128,64]{2,0,1:T(2,128)S(1)} all-gather(s32[2,2,64]{2,0,1:T(2,128)S(1)} %copy.31), channel_id=1, replica_groups=mesh['dp'=64,'tensor'=8] {'dp'}, dimensions={1}, use_global_device_ids=true | all-gather | bytes 66560 | tf_op jit(solution)/shard_map/all_gather | solution.py:26
  66.3 7.2 copy.36
  73.8 59.7 %gather_fusion = bf16[16384,32]{1,0:T(8,128)(2,1)} fusion(bf16[32,31264]{0,1:T(8,128)(2,1)} %copy.36, s32[16384]{0:T(1024)S(1)} %broadcast_clamp_fusion), kind=kCustom, calls=%fused_computation | custom fusion | bytes 2162688 | tf_op jit(solution)/shard_map/jit(_take)/gather | solution.py:32
  133.5 13.9 %select_select_fusion = bf16[16384,32]{1,0:T(8,128)(2,1)} fusion(bf16[16384,32]{1,0:T(8,128)(2,1)} %gather_fusion, pred[16384]{0:T(1024)(128)(4,1)S(1)} %and.19, pred[16384]{0:T(1024)(128)(4,1)S(1)} %compare_and_fusion), kind=kLoop, calls=%fused_computation.2 | loop fusion | flops 1048576 | bytes 2129920 | tf_op jit(solution)/shard_map/jit(_where)/select_n | solution.py:33
  147.4 5.6 copy.37
  154.2 72.8 %all-reduce.5.cloned.1.call-done = bf16[32,2,64,128]{3,1,0,2:T(2,128)(2,1)} async-done(((bf16[32,2,64,128]{3,1,0,2:T(2,128)(2,1)}), bf16[32,2,64,128]{3,1,0,2:T(2,128)(2,1)}) %all-reduce.5.cloned.1.call-update) | async-done | bytes 1048592 | tf_op jit(solution)/shard_map/psum | solution.py:34
  227.0 14.6 %all-to-all-start = ((bf16[32,2,64,128]{3,1,0,2:T(2,128)(2,1)}), bf16[32,2,64,128]{3,1,0,2:T(2,128)(2,1)S(1)}, u32[]{:S(2)}, u32[]{:S(2)}) async-start(bf16[32,2,64,128]{3,1,0,2:T(2,128)(2,1)} %all-reduce.5.cloned.1.call-done), calls=%async_computation | async-start | bytes 2097152 | tf_op jit(solution)/shard_map/all_to_all | solution.py:36
  242.2 28.4 %all-to-all-done = bf16[32,2,64,128]{3,1,0,2:T(2,128)(2,1)S(1)} async-done(((bf16[32,2,64,128]{3,1,0,2:T(2,128)(2,1)}), bf16[32,2,64,128]{3,1,0,2:T(2,128)(2,1)S(1)}, u32[]{:S(2)}, u32[]{:S(2)}) %all-to-all-start) | async-done | bytes 1048608 | tf_op jit(solution)/shard_map/all_to_all | solution.py:36
  271.5 1.5 copy.59
  273.0 1.9 copy.38
  276.0 2.1 fusion.44
  278.1 43.5 %all-gather.9.cloned.1.call-done = bf16[384,2048]{0,1:T(8,128)(2,1)} async-done(((bf16[384,32]{0,1:T(8,128)(2,1)}), bf16[384,2048]{0,1:T(8,128)(2,1)}) %all-gather.9.cloned.1.call-update) | async-done | bytes 1572880 | tf_op jit(solution)/shard_map/all_gather | solution.py:48
  321.6 83.7 %all-gather.7.cloned.1.call-done = bf16[2048,384]{1,0:T(8,128)(2,1)} async-done(((bf16[32,384]{1,0:T(8,128)(2,1)}), bf16[2048,384]{1,0:T(8,128)(2,1)}) %all-gather.7.cloned.1.call-update) | async-done | bytes 1572880 | tf_op jit(solution)/shard_map/all_gather | solution.py:44
  405.3 4.6 fusion.12
  410.6 80.6 %all-reduce.7.cloned.1.call-done = f32[256,2048]{1,0:T(8,128)} async-done(((f32[256,2048]{1,0:T(8,128)}), f32[256,2048]{1,0:T(8,128)}) %all-reduce.7.cloned.1.call-update) | async-done | bytes 2097168 | tf_op jit(solution)/shard_map/psum | solution.py:50
  491.2 1.8 bitcast_add_fusion
  494.2 55.6 %all-gather = bf16[1,128,2048]{2,0,1:T(2,128)(2,1)S(1)} all-gather(bf16[1,2,2048]{2,0,1:T(2,128)(2,1)S(1)} %copy.39), channel_id=2, replica_groups=mesh['dp'=64,'tensor'=8] {'dp'}, dimensions={1}, use_global_device_ids=true | all-gather | bytes 532480 | tf_op jit(solution)/shard_map/all_gather | solution.py:70
  550.9 1.4 convolution_multiply_fusion
  552.5 1.3 dynamic-slice
  554.4 1.6 fusion.5
  556.1 186.8 %all-reduce.9.cloned.1.call-done = f32[128,2048]{1,0:T(8,128)} async-done(((f32[128,2048]{1,0:T(8,128)}), f32[128,2048]{1,0:T(8,128)}) %all-reduce.9.cloned.1.call-update) | async-done | bytes 1048592
  745.0 4.3 fusion.13
  749.3 127.1 %psum.23 = f32[]{:T(128)} all-reduce(f32[]{:T(128)} %get-tuple-element.11), channel_id=1, replica_groups=mesh['dp'=64,'tensor'=8] {'dp'}, use_global_device_ids=true, to_apply=%region_7.8 | all-reduce | flops 1 | bytes 8 | tf_op jit(solution)/shard_map/psum | solution.py:75
  877.1 16.8 %reduce-scatter.2.cloned.1.call-done = f32[32,384]{1,0:T(8,128)} async-done(((f32[2048,384]{1,0:T(8,128)}), f32[32,384]{1,0:T(8,128)}) %reduce-scatter.2.cloned.1.call-update) | async-done | bytes 49168 | tf_op jit(solution)/shard_map/reduce_scatter | solution.py:97
  (55 shorter events, 10.3 us)
Async XLA Ops:
  8.0 219.0 %all-reduce.5.cloned.1.call-start = ((), (), s32[]{:S(2)}) async-start(), calls=%async_computation.2 | async-start | bytes 2097152 | tf_op jit(solution)/shard_map/psum | solution.py:34
  153.0 122.9 %all-gather.5.cloned.1.call-start = ((), (), s32[]{:S(2)}) async-start(), calls=%async_computation.3 | async-start | bytes 1597440 | tf_op jit(solution)/shard_map/all_gather | solution.py:41
  153.6 167.9 %all-gather.9.cloned.1.call-start = ((), (), s32[]{:S(2)}) async-start(), calls=%async_computation.5 | async-start | bytes 1597440 | tf_op jit(solution)/shard_map/all_gather | solution.py:48
  227.0 43.7 %all-to-all-start = ((bf16[32,2,64,128]{3,1,0,2:T(2,128)(2,1)}), bf16[32,2,64,128]{3,1,0,2:T(2,128)(2,1)S(1)}, u32[]{:S(2)}, u32[]{:S(2)}) async-start(bf16[32,2,64,128]{3,1,0,2:T(2,128)(2,1)} %all-reduce.5.cloned.1.call-done), calls=%async_computation | async-start | bytes 2097152 | tf_op jit(solution)/shard_map/all_to_all | solution.py:36
  241.6 163.7 %all-gather.7.cloned.1.call-start = ((), (), s32[]{:S(2)}) async-start(), calls=%async_computation.4 | async-start | bytes 1597440 | tf_op jit(solution)/shard_map/all_gather | solution.py:44
  242.2 249.0 %all-reduce.7.cloned.1.call-start = ((), (), s32[]{:S(2)}) async-start(), calls=%async_computation.6 | async-start | bytes 4194304 | tf_op jit(solution)/shard_map/psum | solution.py:50
  275.0 0.7 copy-start.2
  409.9 0.7 copy-start.3
  409.9 332.9 %all-reduce.9.cloned.1.call-start = ((), (), s32[]{:S(2)}) async-start(), calls=%async_computation.8 | async-start | bytes 2097152
  493.1 56.7 %copy-start.4 = (s32[2]{0:T(128)S(1)}, s32[2]{0:T(128)}, u32[]{:S(2)}) copy-start(s32[2]{0:T(128)} %param.10) | copy-start | bytes 28
  549.8 1.1 copy-start.1
  550.9 194.0 %copy-start = (bf16[384,2048]{0,1:T(8,128)(2,1)S(1)}, bf16[384,2048]{0,1:T(8,128)(2,1)}, u32[]{:S(2)}) copy-start(bf16[384,2048]{0,1:T(8,128)(2,1)} %all-gather.9.cloned.1.call-done) | copy-start | bytes 4718596
  552.4 341.5 %reduce-scatter.2.cloned.1.call-start = ((), (), s32[]{:S(2)}) async-start(), calls=%async_computation.7 | async-start | bytes 3194880 | tf_op jit(solution)/shard_map/reduce_scatter | solution.py:97
Sparse Core Ops, SparseCore 0:
  153.2 73.7 all-reduce.4
  410.0 81.1 all-reduce.6
Sparse Core Ops, SparseCore 1:
  156.8 79.8 all-gather.4
  239.9 81.5 all-gather.8
  324.8 80.5 all-gather.6
  552.5 190.3 all-reduce.8
  749.4 144.4 reduce-scatter.1
where the time goes:
time: 908 us; the launch traced here: 903 us
  waiting for transfers between devices  514 us (57%)
  blocking collectives  240 us (26%)
  local copies, waits for them, and re-layouts  80.5 us (9%)
  other arithmetic  19.5 us (2%)
  between operations  18.3 us (2%)
  matrix products  15.4 us (2%)
  starting transfers between devices  14.9 us (2%)
    unnamed x8, waiting for transfers between devices  188 us
    psum x1, blocking collectives, on_device(): ce_total = lax.psum(jnp.sum(log_total - chosen), 'dp')  127 us
    all_gather x1, waiting for transfers between devices, on_device(): lax.all_gather(w_up, 'dp', axis=0, tiled=True)  83.7 us
    psum x1, waiting for transfers between devices, on_device(): states = resid + lax.psum(partial_out, 'tensor')  80.6 us
    psum x1, waiting for transfers between devices, on_device(): summed = lax.psum(masked, 'tensor').astype(jnp.float32).astype(jnp.bfloat16)  72.8 us
    gather x1, local copies, waits for them, and re-layouts, on_device(): picked = jnp.take(embed_table, safe_ids, axis=1)  59.7 us
    all_gather x1, blocking collectives, on_device(): lax.all_gather(token_ids, 'dp', axis=1, tiled=True)  57 us
    all_gather x1, blocking collectives, on_device(): passages = lax.all_gather(reps[1], 'dp', axis=0, tiled=True)  55.6 us
  transfers between devices with their start and end apart: 8, of which 7 were waited for; matrix products, arithmetic and copies ran while one was open for 1% of the time, Pallas kernels for 0%

commit v1 on v0

v1 whole, which is shorter than its diff:
```python
import jax
import jax.numpy as jnp
from jax import lax
from jax.sharding import PartitionSpec as P

score_scale = 20.0


def product(left, right, left_dim, right_dim):
    return lax.dot_general(
        left, right, (((left_dim,), (right_dim,)), ((), ())), preferred_element_type=jnp.float32
    )


def gather_all(block, axis):
    count = lax.axis_size(axis)
    copies = jnp.broadcast_to(block[None], (count,) + block.shape)
    return lax.all_to_all(copies, axis, 0, 0, tiled=True)


def on_device(token_ids, lengths, positives, embed_table, norm_gain, w_gate, w_up, w_down):
    dp_count = lax.axis_size("dp")
    tensor_count = lax.axis_size("tensor")
    pair_dev = token_ids.shape[1]
    seq_len = token_ids.shape[2]
    feats, vocab_block = embed_table.shape
    width = feats * dp_count
    units = w_gate.shape[1]
    pair_total = pair_dev * dp_count
    tokens = 2 * pair_dev * seq_len
    part = feats // tensor_count

    with jax.named_scope("weights"):
        rows = jnp.concatenate([w_gate, w_up, w_down.T], axis=1)
        weights = lax.all_gather(rows, "dp", axis=0, tiled=True)

    with jax.named_scope("ids"):
        flat = jnp.concatenate([token_ids.reshape(-1), positives])
        flat = jnp.pad(flat, (0, -flat.shape[0] % 128)).reshape(-1, 128)
        arrived = gather_all(flat, "dp").reshape(dp_count, -1)
        all_ids = arrived[:, :tokens]
        all_pos = arrived[:, tokens : tokens + pair_dev].reshape(-1)

    with jax.named_scope("lookup"):
        local_ids = all_ids.reshape(-1) - lax.axis_index("tensor") * vocab_block
        inside = (local_ids >= 0) & (local_ids < vocab_block)
        safe_ids = jnp.clip(local_ids, 0, vocab_block - 1)
        picked = jnp.take(embed_table, safe_ids, axis=1)
        picked = jnp.where(inside[None, :], picked, jnp.zeros((), picked.dtype))

    with jax.named_scope("embed_exchange"):
        blocks = picked.reshape(tensor_count, part, dp_count, tokens).transpose(2, 0, 1, 3)
        blocks = blocks.reshape(dp_count * tensor_count, part, tokens)
        blocks = lax.all_to_all(blocks, ("dp", "tensor"), 0, 0, tiled=True)
        blocks = blocks.reshape(dp_count, tensor_count, part, tokens)
        mine = jnp.sum(blocks.astype(jnp.float32), axis=1).astype(jnp.bfloat16)
        mine = mine.reshape(dp_count * part, tokens)
        full = gather_all(mine, "tensor").reshape(tensor_count, dp_count, part, tokens)
        embedded = full.transpose(1, 0, 2, 3).reshape(width, tokens)

    with jax.named_scope("forward"):
        resid = embedded.astype(jnp.float32)
        scale = lax.rsqrt(jnp.mean(resid * resid, axis=0, keepdims=True) + 1e-06)
        normed = (resid * scale * norm_gain[:, None]).astype(jnp.bfloat16)
        gate_proj = product(weights[:, :units], normed, 0, 0)
        up_proj = product(weights[:, units : 2 * units], normed, 0, 0)
        down = weights[:, 2 * units :]
        activated = jax.nn.gelu(gate_proj, approximate=True)
        hidden = (activated * up_proj).astype(jnp.bfloat16)

    with jax.named_scope("pool"):
        seq_lens = lengths.reshape(-1).astype(jnp.float32)
        positions = jnp.arange(seq_len, dtype=jnp.int32)
        pad_mask = (positions[None, :] < lengths.reshape(-1)[:, None]).astype(jnp.float32)
        sentences = 2 * pair_dev
        hidden_sum = jnp.sum(
            hidden.astype(jnp.float32).reshape(units, sentences, seq_len) * pad_mask[None], axis=2
        )
        resid_sum = jnp.sum(resid.reshape(width, sentences, seq_len) * pad_mask[None], axis=2)
        high = hidden_sum.astype(jnp.bfloat16)
        low = (hidden_sum - high.astype(jnp.float32)).astype(jnp.bfloat16)
        both = product(jnp.concatenate([high, low], axis=1), down, 0, 1)
        partial_out = both[:sentences] + both[sentences:]
        out_sum = jnp.sum(gather_all(partial_out, "tensor"), axis=0)
        pooled = (resid_sum.T + out_sum) / seq_lens[:, None]
        inv_rms = lax.rsqrt(jnp.mean(pooled * pooled, axis=-1, keepdims=True) + 1e-06)
        reps = (pooled * inv_rms).astype(jnp.bfloat16)

    with jax.named_scope("scores"):
        all_reps = gather_all(reps, "dp")
        queries = all_reps[:, :pair_dev].reshape(pair_total, width)
        passages = all_reps[:, pair_dev:].reshape(pair_total, width)
        factor = score_scale / width
        scores = factor * product(queries, passages, 1, 1)
        log_total = jnp.log(jnp.sum(jnp.exp(scores), axis=1, keepdims=True))
        columns = jnp.arange(pair_total, dtype=jnp.int32)
        one_hot = (columns[None, :] == all_pos[:, None]).astype(jnp.float32)
        chosen = jnp.sum(scores * one_hot, axis=1, keepdims=True)
        loss = jnp.sum(log_total - chosen) / pair_total
        coef = (jnp.exp(scores - log_total) - one_hot).astype(jnp.bfloat16)
        first = lax.axis_index("dp") * pair_dev
        coef_rows = lax.dynamic_slice_in_dim(coef, first, pair_dev, 0)
        coef_columns = lax.dynamic_slice_in_dim(coef, first, pair_dev, 1)
        grad_query = factor * product(coef_rows, passages, 1, 0)
        grad_passage = factor * product(coef_columns, queries, 0, 0)

    with jax.named_scope("backward"):
        grad_reps = jnp.concatenate([grad_query, grad_passage])
        grad_pooled = (
            inv_rms * grad_reps
            - pooled * inv_rms**3 * jnp.sum(grad_reps * pooled, axis=-1, keepdims=True) / width
        )
        token_grad = (grad_pooled / seq_lens[:, None]).astype(jnp.bfloat16)
        d_hidden = product(down, token_grad, 0, 1)
        d_tokens = (d_hidden[:, :, None] * pad_mask[None]).reshape(units, tokens)
        d_up = (d_tokens * activated).astype(jnp.bfloat16)
        partial_grad = product(normed, d_up, 1, 1).astype(jnp.bfloat16)
        parts = lax.all_to_all(
            partial_grad.reshape(dp_count, feats, units), "dp", 0, 0, tiled=True
        )
        grad_up = jnp.sum(parts.astype(jnp.float32), axis=0)
    return (loss, grad_up)


def solution(mesh):
    in_specs = (
        P(None, "dp", None),
        P(None, "dp"),
        P("dp"),
        P("dp", "tensor"),
        P(),
        P("dp", "tensor"),
        P("dp", "tensor"),
        P("tensor", "dp"),
    )
    out_specs = (P(), P("dp", "tensor"))
    return jax.shard_map(
        on_device, mesh=mesh, in_specs=in_specs, out_specs=out_specs, check_vma=False
    )
```

time: 908 us -> 307 us (0.34)
  waiting for transfers between devices: 514 us -> 95.5 us
  blocking collectives: 240 us -> 47.7 us
  starting transfers between devices: 14.9 us -> 37.6 us
    unnamed x8 -> x1, waiting for transfers between devices: 188 us -> 0.02 us
    psum x2 -> x0, waiting for transfers between devices: 153 us -> none  [the longest x1 80.6 us: on_device(): states = resid + lax.psum(partial_out, 'tensor')]
    all_gather x3 -> x1, waiting for transfers between devices: 127 us -> 0.02 us  [on_device(): weights = lax.all_gather(rows, 'dp', axis=0, tiled=True)]
    psum x1 -> x0, blocking collectives: 127 us -> none  [on_device(): ce_total = lax.psum(jnp.sum(log_total - chosen), 'dp')]
    all_gather x2 -> x0, blocking collectives: 113 us -> none  [the longest x1 57 us: on_device(): lax.all_gather(token_ids, 'dp', axis=1, tiled=True)]
    all_to_all x1 -> x5, waiting for transfers between devices: 28.4 us -> 95.4 us  [the longest x4 56.3 us: gather_all(): return lax.all_to_all(copies, axis, 0, 0, tiled=True)]
    all_to_all x0 -> x1, blocking collectives: none -> 47.7 us  [on_device(): blocks = lax.all_to_all(blocks, ('dp', 'tensor'), 0, 0, tiled=True)]
    all_to_all x1 -> x5, starting transfers between devices: 14.6 us -> 37.6 us  [the longest x4 31.4 us: gather_all(): return lax.all_to_all(copies, axis, 0, 0, tiled=True)]
  transfers between devices with their start and end apart: 8 -> 6, of which waited for: 7 -> 5; matrix products, arithmetic and copies ran while one was open for 1% -> 30% of each run, Pallas kernels for 0% -> 0%
where the time goes in v1:
time: 307 us; the launch traced here: 306 us
  waiting for transfers between devices  95.5 us (31%)
  local copies, waits for them, and re-layouts  86.3 us (28%)
  blocking collectives  47.7 us (16%)
  starting transfers between devices  37.6 us (12%)
  between operations  16.1 us (5%)
  other arithmetic  14.8 us (5%)
  matrix products  8.08 us (3%)
    gather x2, local copies, waits for them, and re-layouts, on_device(): picked = jnp.take(embed_table, safe_ids, axis=1)  63.1 us
    all_to_all x4, waiting for transfers between devices, gather_all(): return lax.all_to_all(copies, axis, 0, 0, tiled=True)  56.3 us
    all_to_all x1, blocking collectives, on_device(): blocks = lax.all_to_all(blocks, ('dp', 'tensor'), 0, 0, tiled=True)  47.7 us
    all_to_all x1, waiting for transfers between devices, on_device(): lax.all_to_all(partial_grad.reshape(dp_count, feats, units), 'dp', 0, 0,...  39.2 us
    all_to_all x4, starting transfers between devices, gather_all(): return lax.all_to_all(copies, axis, 0, 0, tiled=True)  31.4 us
    dot_general x8, matrix products, product(): lax.dot_general(left, right, (((left_dim,), (right_dim,)), ((), ())), pre...  8.08 us
    unnamed x18, local copies, waits for them, and re-layouts  7.97 us
    convert_element_type x3, local copies, waits for them, and re-layouts, on_device(): resid = embedded.astype(jnp.float32)  6.37 us
  transfers between devices with their start and end apart: 6, of which 5 were waited for; matrix products, arithmetic and copies ran while one was open for 30% of the time, Pallas kernels for 0%

profile of v1, /device:TPU:1, one launch (start us, length us, event | category | flops | bytes accessed | tf_op | source)
XLA Modules:
  0.0 306.1 jit_solution(11216985179757954843)
XLA Ops:
  9.3 14.8 %all-to-all-start = ((s32[64,3,128]{2,1,0:T(4,128)}), s32[64,3,128]{2,1,0:T(4,128)S(1)}, u32[]{:S(2)}, u32[]{:S(2)}) async-start(s32[64,3,128]{2,1,0:T(4,128)} %broadcast_in_dim.35), calls=%async_computation | async-start | bytes 262144 | tf_op jit(solution)/shard_map/ids/all_to_all | solution.py:18
  24.2 1.4 pad_maximum_fusion
  25.6 7.2 %copy.48 = bf16[32,31264]{0,1:T(8,128)(2,1)} copy(bf16[32,31264]{1,0:T(8,128)(2,1)} %param.11) | data formatting | bytes 4001792 | tf_op args[3]
  32.8 1.7 all-to-all-done
  34.7 59.7 %gather_fusion = bf16[16384,32]{1,0:T(8,128)(2,1)} fusion(bf16[32,31264]{0,1:T(8,128)(2,1)} %copy.48, s32[16384]{0:T(1024)S(1)} %broadcast_clamp_fusion), kind=kCustom, calls=%fused_computation | custom fusion | bytes 2162688 | tf_op jit(solution)/shard_map/lookup/jit(_take)/gather | solution.py:48
  94.3 3.5 %copy.49 = bf16[32,16384]{1,0:T(8,128)(2,1)S(1)} copy(bf16[32,16384]{0,1:T(8,128)(2,1)} %bitcast.51) | data formatting | bytes 2097152 | tf_op jit(solution)/shard_map/lookup/jit(_take)/gather | solution.py:48
  99.7 47.7 %all_to_all.30 = bf16[512,4,256]{2,1,0:T(4,128)(2,1)S(1)} all-to-all(bf16[512,4,256]{2,1,0:T(4,128)(2,1)S(1)} %copy.51), channel_id=1, replica_groups=mesh['dp'=64,'tensor'=8] {'dp','tensor'}, dimensions={0} | all-to-all | bytes 2097152 | tf_op jit(solution)/shard_map/embed_exchange/all_to_all | solution.py:54
  148.0 1.1 broadcast_in_dim.41
  149.1 3.7 %all-to-all-start.2 = ((bf16[8,256,256]{2,1,0:T(8,128)(2,1)}), bf16[8,256,256]{2,1,0:T(8,128)(2,1)S(1)}, u32[]{:S(2)}, u32[]{:S(2)}) async-start(bf16[8,256,256]{2,1,0:T(8,128)(2,1)} %broadcast_in_dim.41), calls=%async_computation.2 | async-start | bytes 2097152 | tf_op jit(solution)/shard_map/embed_exchange/all_to_all | solution.py:18
  153.0 26.8 %all-to-all-done.2 = bf16[8,256,256]{2,1,0:T(8,128)(2,1)S(1)} async-done(((bf16[8,256,256]{2,1,0:T(8,128)(2,1)}), bf16[8,256,256]{2,1,0:T(8,128)(2,1)S(1)}, u32[]{:S(2)}, u32[]{:S(2)}) %all-to-all-start.2) | async-done | bytes 1048608 | tf_op jit(solution)/shard_map/embed_exchange/all_to_all | solution.py:18
  181.4 1.8 reshape.185
  183.7 1.9 multiply_convert_fusion
  185.7 2.4 fusion.20
  190.6 4.0 %all-to-all-start.3 = ((f32[8,4,2048]{2,1,0:T(4,128)}), f32[8,4,2048]{2,1,0:T(4,128)}, u32[]{:S(2)}, u32[]{:S(2)}) async-start(f32[8,4,2048]{2,1,0:T(4,128)} %broadcast_in_dim.42), calls=%async_computation.3 | async-start | bytes 524288 | tf_op jit(solution)/shard_map/pool/all_to_all | solution.py:18
  194.7 3.6 %reshape.184 = f32[2048,4,64]{2,1,0:T(4,128)} reshape(f32[64,8,4,256]{3,2,1,0:T(4,128)S(1)} %copy.55) | data formatting | bytes 4194304 | tf_op jit(solution)/shard_map/forward/convert_element_type | solution.py:62
  198.3 5.0 %multiply_reduce_fusion = f32[2048,4]{1,0:T(8,128)S(1)} fusion(f32[2048,4,64]{2,1,0:T(4,128)} %reshape.184, f32[4,64]{1,0:T(4,128)S(1)} %fusion.38), kind=kLoop, calls=%fused_computation.1 | loop fusion | flops 1040384 | bytes 2130944 | tf_op jit(solution)/shard_map/pool/reduce_sum | solution.py:79
  204.0 1.0 reduce_sum.106
  205.9 1.5 broadcast_in_dim.72
  207.4 8.8 %all-to-all-start.4 = ((bf16[64,4,2048]{2,1,0:T(4,128)(2,1)}), bf16[64,4,2048]{2,1,0:T(4,128)(2,1)S(1)}, u32[]{:S(2)}, u32[]{:S(2)}) async-start(bf16[64,4,2048]{2,1,0:T(4,128)(2,1)} %broadcast_in_dim.72), calls=%async_computation.4 | async-start | bytes 2097152 | tf_op jit(solution)/shard_map/scores/all_to_all | solution.py:18
  217.3 27.4 %all-to-all-done.4 = bf16[64,4,2048]{2,1,0:T(4,128)(2,1)S(1)} async-done(((bf16[64,4,2048]{2,1,0:T(4,128)(2,1)}), bf16[64,4,2048]{2,1,0:T(4,128)(2,1)S(1)}, u32[]{:S(2)}, u32[]{:S(2)}) %all-to-all-start.4) | async-done | bytes 1048608 | tf_op jit(solution)/shard_map/scores/all_to_all | solution.py:18
  247.5 1.8 fusion.4
  249.4 1.9 convolution_convert_fusion
  251.2 6.2 %all-to-all-start.5 = ((bf16[64,32,384]{2,1,0:T(8,128)(2,1)}), bf16[64,32,384]{2,1,0:T(8,128)(2,1)S(1)}, u32[]{:S(2)}, u32[]{:S(2)}) async-start(bf16[64,32,384]{2,1,0:T(8,128)(2,1)} %bitcast.13), calls=%async_computation.5 | async-start | bytes 3145728 | tf_op jit(solution)/shard_map/backward/all_to_all | solution.py:118
  258.0 39.2 %all-to-all-done.5 = bf16[64,32,384]{2,1,0:T(8,128)(2,1)S(1)} async-done(((bf16[64,32,384]{2,1,0:T(8,128)(2,1)}), bf16[64,32,384]{2,1,0:T(8,128)(2,1)S(1)}, u32[]{:S(2)}, u32[]{:S(2)}) %all-to-all-start.5) | async-done | bytes 1572896 | tf_op jit(solution)/shard_map/backward/all_to_all | solution.py:118
  (68 shorter events, 16.0 us)
Async XLA Ops:
  9.3 25.2 %all-to-all-start = ((s32[64,3,128]{2,1,0:T(4,128)}), s32[64,3,128]{2,1,0:T(4,128)S(1)}, u32[]{:S(2)}, u32[]{:S(2)}) async-start(s32[64,3,128]{2,1,0:T(4,128)} %broadcast_in_dim.35), calls=%async_computation | async-start | bytes 262144 | tf_op jit(solution)/shard_map/ids/all_to_all | solution.py:18
  24.1 161.6 %all-gather.2.cloned.1.call-start = ((), (), s32[]{:S(2)}) async-start(), calls=%async_computation.6 | async-start | bytes 4792320 | tf_op jit(solution)/shard_map/weights/all_gather | solution.py:35
  34.5 63.6 %copy-start.1 = (s32[8,8,3,128]{3,1,2,0:T(8,128)}, s32[8,8,3,128]{3,1,2,0:T(8,128)S(1)}, u32[]{:S(2)}) copy-start(s32[8,8,3,128]{3,1,2,0:T(8,128)S(1)} %copy.70) | copy-start | bytes 294916
  147.4 5.5 %copy-start.5 = (s32[2,2]{1,0:T(2,128)S(1)}, s32[2,2]{1,0:T(2,128)}, u32[]{:S(2)}) copy-start(s32[2,2]{1,0:T(2,128)} %param.9) | copy-start | bytes 52
  149.1 30.7 %all-to-all-start.2 = ((bf16[8,256,256]{2,1,0:T(8,128)(2,1)}), bf16[8,256,256]{2,1,0:T(8,128)(2,1)S(1)}, u32[]{:S(2)}, u32[]{:S(2)}) async-start(bf16[8,256,256]{2,1,0:T(8,128)(2,1)} %broadcast_in_dim.41), calls=%async_computation.2 | async-start | bytes 2097152 | tf_op jit(solution)/shard_map/embed_exchange/all_to_all | solution.py:18
  181.4 2.4 copy-start.4
  185.7 2.8 copy-start
  190.6 13.4 %all-to-all-start.3 = ((f32[8,4,2048]{2,1,0:T(4,128)}), f32[8,4,2048]{2,1,0:T(4,128)}, u32[]{:S(2)}, u32[]{:S(2)}) async-start(f32[8,4,2048]{2,1,0:T(4,128)} %broadcast_in_dim.42), calls=%async_computation.3 | async-start | bytes 524288 | tf_op jit(solution)/shard_map/pool/all_to_all | solution.py:18
  205.2 2.1 copy-start.2
  207.4 37.3 %all-to-all-start.4 = ((bf16[64,4,2048]{2,1,0:T(4,128)(2,1)}), bf16[64,4,2048]{2,1,0:T(4,128)(2,1)S(1)}, u32[]{:S(2)}, u32[]{:S(2)}) async-start(bf16[64,4,2048]{2,1,0:T(4,128)(2,1)} %broadcast_in_dim.72), calls=%async_computation.4 | async-start | bytes 2097152 | tf_op jit(solution)/shard_map/scores/all_to_all | solution.py:18
  245.6 1.7 copy-start.3
  245.6 1.9 copy-start.6
  251.2 46.0 %all-to-all-start.5 = ((bf16[64,32,384]{2,1,0:T(8,128)(2,1)}), bf16[64,32,384]{2,1,0:T(8,128)(2,1)S(1)}, u32[]{:S(2)}, u32[]{:S(2)}) async-start(bf16[64,32,384]{2,1,0:T(8,128)(2,1)} %bitcast.13), calls=%async_computation.5 | async-start | bytes 3145728 | tf_op jit(solution)/shard_map/backward/all_to_all | solution.py:118
Sparse Core Ops, SparseCore 0:
  28.3 86.9 all-gather.1

commit v2 on v1

--- a/solution.py
+++ b/solution.py
@@ -1,9 +1,14 @@
+import functools
+
 import jax
 import jax.numpy as jnp
 from jax import lax
+from jax.experimental import pallas as pl
+from jax.experimental.pallas import tpu as pltpu
 from jax.sharding import PartitionSpec as P
 
 score_scale = 20.0
+lanes = 128
 
 
 def product(left, right, left_dim, right_dim):
@@ -16,6 +21,88 @@
     count = lax.axis_size(axis)
     copies = jnp.broadcast_to(block[None], (count,) + block.shape)
     return lax.all_to_all(copies, axis, 0, 0, tiled=True)
+
+
+def pack_kernel(span, table_ref, rows_ref):
+    feats, vocab = table_ref.shape
+    slots = lanes // feats
+
+    def piece(slot, start, wide):
+        return table_ref[:, pl.ds(slot * span + start, wide)].astype(jnp.float32)
+
+    whole = (vocab - (slots - 1) * span) // lanes
+
+    @pl.loop(0, whole)
+    def _(step):
+        start = pl.multiple_of(step * lanes, lanes)
+        stacked = jnp.concatenate([piece(slot, start, lanes) for slot in range(slots)], axis=0)
+        rows_ref[pl.ds(start, lanes), :] = stacked.T
+
+    for step in range(whole, span // lanes):
+        start = step * lanes
+        left = max(0, vocab - (slots - 1) * span - start)
+        last = jnp.zeros((feats, lanes - left), jnp.float32)
+        if left:
+            last = jnp.concatenate([piece(slots - 1, start, left), last], axis=1)
+        stacked = jnp.concatenate([piece(slot, start, lanes) for slot in range(slots - 1)] + [last], axis=0)
+        rows_ref[start : start + lanes, :] = stacked.T
+
+
+def pick_kernel(row_ref, slot_ref, rows_ref, out_ref, held_ref):
+    groups, tokens = row_ref.shape
+    feats = out_ref.shape[1]
+    slots = lanes // feats
+
+    @pl.loop(0, groups)
+    def _(group):
+        for token in range(tokens):
+            held_ref[pl.ds(token, 1), :] = rows_ref[pl.ds(row_ref[group, token], 1), :]
+        slot = slot_ref[pl.ds(group, 1), :]
+        for first in range(0, tokens, lanes):
+            turned = held_ref[first : first + lanes, :].T
+            mine = slot[:, first : first + lanes]
+            total = jnp.zeros((feats, lanes), jnp.float32)
+            for index in range(slots):
+                total += jnp.where(mine == index, turned[index * feats : (index + 1) * feats], 0.0)
+            out_ref[group, :, first : first + lanes] = total.astype(out_ref.dtype)
+
+
+def pack_table(table):
+    feats, vocab = table.shape
+    slots = lanes // feats
+    span = -(-vocab // (slots * lanes)) * lanes
+    return pl.pallas_call(
+        functools.partial(pack_kernel, span),
+        out_shape=jax.ShapeDtypeStruct((span, lanes), jnp.float32),
+        in_specs=[pl.BlockSpec(memory_space=pltpu.VMEM)],
+        out_specs=pl.BlockSpec(memory_space=pltpu.VMEM),
+        compiler_params=pltpu.CompilerParams(vmem_limit_bytes=32 << 20),
+        cost_estimate=pl.CostEstimate(flops=0, bytes_accessed=3 * feats * vocab * 2, transcendentals=0),
+    )(table)
+
+
+def pick_rows(rows, packed, feats):
+    slots = lanes // feats
+    span = packed.shape[0]
+    groups, tokens = rows.shape
+    inside = (rows >= 0) & (rows < slots * span)
+    safe = jnp.where(inside, rows, 0)
+    slot = safe // span
+    row = safe - slot * span
+    slot = jnp.where(inside, slot, slots)
+    return pl.pallas_call(
+        pick_kernel,
+        out_shape=jax.ShapeDtypeStruct((groups, feats, tokens), jnp.bfloat16),
+        in_specs=[
+            pl.BlockSpec(memory_space=pltpu.SMEM),
+            pl.BlockSpec(memory_space=pltpu.VMEM),
+            pl.BlockSpec(memory_space=pltpu.VMEM),
+        ],
+        out_specs=pl.BlockSpec(memory_space=pltpu.VMEM),
+        scratch_shapes=[pltpu.VMEM((tokens, lanes), jnp.float32)],
+        compiler_params=pltpu.CompilerParams(vmem_limit_bytes=32 << 20),
+        cost_estimate=pl.CostEstimate(flops=0, bytes_accessed=30 << 20, transcendentals=0),
+    )(row, slot, packed)
 
 
 def on_device(token_ids, lengths, positives, embed_table, norm_gain, w_gate, w_up, w_down):
@@ -29,6 +116,8 @@
     pair_total = pair_dev * dp_count
     tokens = 2 * pair_dev * seq_len
     part = feats // tensor_count
+    even_core = lax.axis_index("dp") % 2 == 0
+    swap_cores = [(index, index ^ 1) for index in range(dp_count)]
 
     with jax.named_scope("weights"):
         rows = jnp.concatenate([w_gate, w_up, w_down.T], axis=1)
@@ -42,15 +131,12 @@
         all_pos = arrived[:, tokens : tokens + pair_dev].reshape(-1)
 
     with jax.named_scope("lookup"):
-        local_ids = all_ids.reshape(-1) - lax.axis_index("tensor") * vocab_block
+        local_ids = all_ids - lax.axis_index("tensor") * vocab_block
         inside = (local_ids >= 0) & (local_ids < vocab_block)
-        safe_ids = jnp.clip(local_ids, 0, vocab_block - 1)
-        picked = jnp.take(embed_table, safe_ids, axis=1)
-        picked = jnp.where(inside[None, :], picked, jnp.zeros((), picked.dtype))
+        picked = pick_rows(jnp.where(inside, local_ids, -1), pack_table(embed_table), feats)
 
     with jax.named_scope("embed_exchange"):
-        blocks = picked.reshape(tensor_count, part, dp_count, tokens).transpose(2, 0, 1, 3)
-        blocks = blocks.reshape(dp_count * tensor_count, part, tokens)
+        blocks = picked.reshape(dp_count * tensor_count, part, tokens)
         blocks = lax.all_to_all(blocks, ("dp", "tensor"), 0, 0, tiled=True)
         blocks = blocks.reshape(dp_count, tensor_count, part, tokens)
         mine = jnp.sum(blocks.astype(jnp.float32), axis=1).astype(jnp.bfloat16)
@@ -66,7 +152,7 @@
         up_proj = product(weights[:, units : 2 * units], normed, 0, 0)
         down = weights[:, 2 * units :]
         activated = jax.nn.gelu(gate_proj, approximate=True)
-        hidden = (activated * up_proj).astype(jnp.bfloat16)
+        hidden = lax.reduce_precision(activated * up_proj, 8, 7)
 
     with jax.named_scope("pool"):
         seq_lens = lengths.reshape(-1).astype(jnp.float32)
@@ -74,12 +160,12 @@
         pad_mask = (positions[None, :] < lengths.reshape(-1)[:, None]).astype(jnp.float32)
         sentences = 2 * pair_dev
         hidden_sum = jnp.sum(
-            hidden.astype(jnp.float32).reshape(units, sentences, seq_len) * pad_mask[None], axis=2
+            hidden.reshape(units, sentences, seq_len) * pad_mask[None], axis=2
         )
         resid_sum = jnp.sum(resid.reshape(width, sentences, seq_len) * pad_mask[None], axis=2)
-        high = hidden_sum.astype(jnp.bfloat16)
-        low = (hidden_sum - high.astype(jnp.float32)).astype(jnp.bfloat16)
-        both = product(jnp.concatenate([high, low], axis=1), down, 0, 1)
+        high = lax.reduce_precision(hidden_sum, 8, 7)
+        terms = jnp.concatenate([high, hidden_sum - high], axis=1).astype(jnp.bfloat16)
+        both = product(terms, down, 0, 1)
         partial_out = both[:sentences] + both[sentences:]
         out_sum = jnp.sum(gather_all(partial_out, "tensor"), axis=0)
         pooled = (resid_sum.T + out_sum) / seq_lens[:, None]
@@ -87,11 +173,17 @@
         reps = (pooled * inv_rms).astype(jnp.bfloat16)
 
     with jax.named_scope("scores"):
-        all_reps = gather_all(reps, "dp")
-        queries = all_reps[:, :pair_dev].reshape(pair_total, width)
-        passages = all_reps[:, pair_dev:].reshape(pair_total, width)
+        half = width // 2
+        halves = reps.reshape(2 * pair_dev, 2, half).transpose(1, 0, 2)
+        halves = jnp.broadcast_to(halves[None], (dp_count // 2, 2, 2 * pair_dev, half))
+        mine = lax.all_to_all(
+            halves.reshape(dp_count, 2 * pair_dev, half), "dp", 0, 0, tiled=True
+        )
+        sides = [mine, lax.ppermute(mine, "dp", swap_cores)]
+        queries = [side[:, :pair_dev].reshape(pair_total, half) for side in sides]
+        passages = [side[:, pair_dev:].reshape(pair_total, half) for side in sides]
         factor = score_scale / width
-        scores = factor * product(queries, passages, 1, 1)
+        scores = factor * sum(product(q, p, 1, 1) for q, p in zip(queries, passages))
         log_total = jnp.log(jnp.sum(jnp.exp(scores), axis=1, keepdims=True))
         columns = jnp.arange(pair_total, dtype=jnp.int32)
         one_hot = (columns[None, :] == all_pos[:, None]).astype(jnp.float32)
@@ -101,11 +193,17 @@
         first = lax.axis_index("dp") * pair_dev
         coef_rows = lax.dynamic_slice_in_dim(coef, first, pair_dev, 0)
         coef_columns = lax.dynamic_slice_in_dim(coef, first, pair_dev, 1)
-        grad_query = factor * product(coef_rows, passages, 1, 0)
-        grad_passage = factor * product(coef_columns, queries, 0, 0)
+        grads = [
+            factor * jnp.concatenate([product(coef_rows, p, 1, 0), product(coef_columns, q, 0, 0)])
+            for q, p in zip(queries, passages)
+        ]
+        grad_reps = jnp.where(
+            even_core,
+            jnp.concatenate([grads[0], grads[1]], axis=1),
+            jnp.concatenate([grads[1], grads[0]], axis=1),
+        )
 
     with jax.named_scope("backward"):
-        grad_reps = jnp.concatenate([grad_query, grad_passage])
         grad_pooled = (
             inv_rms * grad_reps
             - pooled * inv_rms**3 * jnp.sum(grad_reps * pooled, axis=-1, keepdims=True) / width
@@ -114,9 +212,20 @@
         d_hidden = product(down, token_grad, 0, 1)
         d_tokens = (d_hidden[:, :, None] * pad_mask[None]).reshape(units, tokens)
         d_up = (d_tokens * activated).astype(jnp.bfloat16)
-        partial_grad = product(normed, d_up, 1, 1).astype(jnp.bfloat16)
+        by_core = normed.reshape(dp_count // 2, 2, feats, tokens)
+        own_rows = jnp.where(even_core, by_core[:, 0], by_core[:, 1]).reshape(-1, tokens)
+        other_rows = jnp.where(even_core, by_core[:, 1], by_core[:, 0]).reshape(-1, tokens)
+        sent = product(other_rows, d_up, 1, 1).astype(jnp.bfloat16)
+        got = lax.ppermute(sent, "dp", swap_cores)
+        partial_grad = (product(own_rows, d_up, 1, 1) + got.astype(jnp.float32)).astype(jnp.bfloat16)
+        same_core = [list(range(core, dp_count, 2)) for core in range(2)]
         parts = lax.all_to_all(
-            partial_grad.reshape(dp_count, feats, units), "dp", 0, 0, tiled=True
+            partial_grad.reshape(dp_count // 2, feats, units),
+            "dp",
+            0,
+            0,
+            tiled=True,
+            axis_index_groups=same_core,
         )
         grad_up = jnp.sum(parts.astype(jnp.float32), axis=0)
     return (loss, grad_up)

time: 307 us -> 256 us (0.83)
  local copies, waits for them, and re-layouts: 86.3 us -> 23.4 us
  waiting for transfers between devices: 95.5 us -> 63.8 us
  Pallas kernels: 0 us -> 31.6 us
  matrix products: 8.08 us -> 13.3 us
    gather x2 -> x0, local copies, waits for them, and re-layouts: 63.1 us -> none  [on_device(): picked = jnp.take(embed_table, safe_ids, axis=1)]
    pallas_call x0 -> x2, Pallas kernels: none -> 31.6 us  [the longest x1 25.7 us: pick_rows(): pl.pallas_call(pick_kernel, out_shape=jax.ShapeDtypeStruct((groups, feats...]
    all_to_all x4 -> x3, waiting for transfers between devices: 56.3 us -> 31.3 us  [gather_all(): return lax.all_to_all(copies, axis, 0, 0, tiled=True)]
    all_to_all x1 -> x2, waiting for transfers between devices: 39.2 us -> 30.5 us  [the longest x1 18.2 us: on_device(): lax.all_to_all(partial_grad.reshape(dp_count // 2, feats, units), 'dp', 0...]
    all_to_all x4 -> x3, starting transfers between devices: 31.4 us -> 23.8 us  [gather_all(): return lax.all_to_all(copies, axis, 0, 0, tiled=True)]
    dot_general x8 -> x12, matrix products: 8.08 us -> 13.3 us  [product(): lax.dot_general(left, right, (((left_dim,), (right_dim,)), ((), ())), pre...]
    all_to_all x1 -> x2, starting transfers between devices: 6.19 us -> 11 us  [the longest x1 5.51 us: on_device(): lax.all_to_all(halves.reshape(dp_count, 2 * pair_dev, half), 'dp', 0, 0,...]
    ppermute x0 -> x2, starting transfers between devices: none -> 4.45 us  [the longest x1 2.23 us: on_device(): got = lax.ppermute(sent, 'dp', swap_cores)]
  transfers between devices with their start and end apart: 6 -> 8, of which waited for: 5 -> 6; matrix products, arithmetic and copies ran while one was open for 30% -> 10% of each run, Pallas kernels for 0% -> 13%
where the time goes in v2:
time: 256 us; the launch traced here: 252 us
  waiting for transfers between devices  63.8 us (25%)
  blocking collectives  48.5 us (19%)
  starting transfers between devices  39.3 us (15%)
  Pallas kernels  31.6 us (12%)
  local copies, waits for them, and re-layouts  23.4 us (9%)
  between operations  16.2 us (6%)
  other arithmetic  15.9 us (6%)
  matrix products  13.3 us (5%)
    all_to_all x1, blocking collectives, on_device(): blocks = lax.all_to_all(blocks, ('dp', 'tensor'), 0, 0, tiled=True)  48.5 us
    all_to_all x3, waiting for transfers between devices, gather_all(): return lax.all_to_all(copies, axis, 0, 0, tiled=True)  31.3 us
    pallas_call x1, Pallas kernels, pick_rows(): pl.pallas_call(pick_kernel, out_shape=jax.ShapeDtypeStruct((groups, feats...  25.7 us
    all_to_all x3, starting transfers between devices, gather_all(): return lax.all_to_all(copies, axis, 0, 0, tiled=True)  23.8 us
    all_to_all x1, waiting for transfers between devices, on_device(): lax.all_to_all(partial_grad.reshape(dp_count // 2, feats, units), 'dp', 0...  18.2 us
    dot_general x12, matrix products, product(): lax.dot_general(left, right, (((left_dim,), (right_dim,)), ((), ())), pre...  13.3 us
    all_to_all x1, waiting for transfers between devices, on_device(): lax.all_to_all(halves.reshape(dp_count, 2 * pair_dev, half), 'dp', 0, 0,...  12.3 us
    convert_element_type x4, local copies, waits for them, and re-layouts, on_device(): resid = embedded.astype(jnp.float32)  8.18 us
  transfers between devices with their start and end apart: 8, of which 6 were waited for; matrix products, arithmetic and copies ran while one was open for 10% of the time, Pallas kernels for 13%

profile of v2, /device:TPU:1, one launch (start us, length us, event | category | flops | bytes accessed | tf_op | source)
XLA Modules:
  0.0 252.0 jit_solution(12412200247302716689)
XLA Ops:
  10.8 14.8 %all-to-all-start = ((s32[64,3,128]{2,1,0:T(4,128)}), s32[64,3,128]{2,1,0:T(4,128)S(1)}, u32[]{:S(2)}, u32[]{:S(2)}) async-start(s32[64,3,128]{2,1,0:T(4,128)} %broadcast_in_dim.21), calls=%async_computation | async-start | bytes 262144 | tf_op jit(solution)/shard_map/ids/all_to_all | solution.py:23
  27.2 6.0 %lookup.2.rows_ref = f32[7936,128]{1,0:T(8,128)S(1)} custom-call(bf16[32,31264]{1,0:T(8,128)(2,1)S(1)} %copy-done.2), custom_call_target="tpu_custom_call" | custom-call | bytes 6002688 | tf_op jit(solution)/shard_map/lookup/pallas_call | solution.py:74
  33.1 2.0 copy-done
  36.6 2.2 copy-done.1
  38.8 25.7 %lookup.3 = bf16[64,32,256]{2,1,0:T(8,128)(2,1)S(1)} custom-call(s32[64,256]{1,0:T(8,128)S(1)} %get-tuple-element.13.row_ref, s32[64,256]{1,0:T(8,128)S(1)} %get-tuple-element.12.slot_ref, f32[7936,128]{1,0:T(8,128)S(1)} %copy-done.1), custom_call_target="tpu_custom_call" | custom-call | bytes 31457280 | tf_op jit(solution)/shard_map/lookup/pallas_call | solution.py:93
  64.8 48.5 %all_to_all.30 = bf16[512,4,256]{2,1,0:T(4,128)(2,1)S(1)} all-to-all(bf16[512,4,256]{2,1,0:T(4,128)(2,1)S(1)} %reshape.159), channel_id=1, replica_groups=mesh['dp'=64,'tensor'=8] {'dp','tensor'}, dimensions={0} | all-to-all | bytes 2097152 | tf_op jit(solution)/shard_map/embed_exchange/all_to_all | solution.py:140
  115.0 4.7 %all-to-all-start.2 = ((bf16[8,256,256]{2,1,0:T(8,128)(2,1)}), bf16[8,256,256]{2,1,0:T(8,128)(2,1)S(1)}, u32[]{:S(2)}, u32[]{:S(2)}) async-start(bf16[8,256,256]{2,1,0:T(8,128)(2,1)} %broadcast_in_dim.25), calls=%async_computation.2 | async-start | bytes 2097152 | tf_op jit(solution)/shard_map/embed_exchange/all_to_all | solution.py:23
  119.9 29.0 %all-to-all-done.2 = bf16[8,256,256]{2,1,0:T(8,128)(2,1)S(1)} async-done(((bf16[8,256,256]{2,1,0:T(8,128)(2,1)}), bf16[8,256,256]{2,1,0:T(8,128)(2,1)S(1)}, u32[]{:S(2)}, u32[]{:S(2)}) %all-to-all-start.2) | async-done | bytes 1048608 | tf_op jit(solution)/shard_map/embed_exchange/all_to_all | solution.py:23
  150.5 1.8 reshape.170
  152.9 3.4 %fusion.21 = f32[384,256]{0,1:T(8,128)S(1)} fusion(bf16[2048,1152]{1,0:T(8,128)(2,1)} %all-gather.2.cloned.1.call-done, f32[2048,256]{1,0:T(8,128)} %reshape.170, f32[2048]{0:T(1024)S(1)} %copy-done.8, f32[256]{0:T(256)S(1)} %add_rsqrt_fusion), kind=kOutput, calls=%fused_computation.30 | convolution fusion | flops 405012480 | bytes 4072448 | tf_op jit(solution)/shard_map/forward/dot_general | solution.py:15
  156.3 2.5 %multiply_reduce_fusion.2 = f32[384,4]{0,1:T(4,128)S(1)} fusion(f32[4,64]{1,0:T(4,128)S(1)} %fusion.44, f32[384,256]{0,1:T(8,128)S(1)} %fusion.21, f32[2048,256]{1,0:T(8,128)S(1)} %copy-done.3, f32[2048]{0:T(1024)S(1)} %copy-done.8, f32[256]{0:T(256)S(1)} %add_rsqrt_fusion, bf16[2048,1152]{1,0:T(8,128)(2,1)} %all-gather.2.cloned.1.call-done), kind=kOutput, calls=%fused_computation.34 | convolution fusion | flops 404617728 | bytes 4079616 | tf_op jit(solution)/shard_map/forward/dot_general | solution.py:15
  158.8 1.9 fusion.6
  161.5 4.2 %all-to-all-start.3 = ((f32[8,4,2048]{2,1,0:T(4,128)}), f32[8,4,2048]{2,1,0:T(4,128)}, u32[]{:S(2)}, u32[]{:S(2)}) async-start(f32[8,4,2048]{2,1,0:T(4,128)} %broadcast_in_dim.26), calls=%async_computation.3 | async-start | bytes 524288 | tf_op jit(solution)/shard_map/pool/all_to_all | solution.py:23
  166.3 3.7 %reshape.169 = f32[2048,4,64]{2,1,0:T(4,128)} reshape(f32[64,8,4,256]{3,2,1,0:T(4,128)S(1)} %copy.29) | data formatting | bytes 4194304 | tf_op jit(solution)/shard_map/forward/convert_element_type | solution.py:148
  170.0 5.0 %multiply_reduce_fusion = f32[2048,4]{1,0:T(8,128)S(1)} fusion(f32[2048,4,64]{2,1,0:T(4,128)} %reshape.169, f32[4,64]{1,0:T(4,128)S(1)} %fusion.44), kind=kLoop, calls=%fused_computation | loop fusion | flops 1040384 | bytes 2130944 | tf_op jit(solution)/shard_map/pool/reduce_sum | solution.py:165
  181.8 5.5 %all-to-all-start.4 = ((bf16[64,4,1024]{2,1,0:T(4,128)(2,1)}), bf16[64,4,1024]{2,1,0:T(4,128)(2,1)S(1)}, u32[]{:S(2)}, u32[]{:S(2)}) async-start(bf16[64,4,1024]{2,1,0:T(4,128)(2,1)} %bitcast.9), calls=%async_computation.4 | async-start | bytes 1048576 | tf_op jit(solution)/shard_map/scores/all_to_all | solution.py:179
  190.3 1.9 multiply_convert_fusion
  192.2 12.3 %all-to-all-done.4 = bf16[64,4,1024]{2,1,0:T(4,128)(2,1)S(1)} async-done(((bf16[64,4,1024]{2,1,0:T(4,128)(2,1)}), bf16[64,4,1024]{2,1,0:T(4,128)(2,1)S(1)}, u32[]{:S(2)}, u32[]{:S(2)}) %all-to-all-start.4) | async-done | bytes 524320 | tf_op jit(solution)/shard_map/scores/all_to_all | solution.py:179
  204.6 2.2 collective-permute-start
  211.2 1.8 fusion.4
  213.5 2.2 collective-permute-start.1
  215.7 1.9 collective-permute-done.1
  219.0 5.5 %all-to-all-start.5 = ((bf16[32,32,384]{2,1,0:T(8,128)(2,1)}), bf16[32,32,384]{2,1,0:T(8,128)(2,1)S(1)}, u32[]{:S(2)}, u32[]{:S(2)}) async-start(bf16[32,32,384]{2,1,0:T(8,128)(2,1)} %bitcast.13), calls=%async_computation.5 | async-start | bytes 1572864 | tf_op jit(solution)/shard_map/backward/all_to_all | solution.py:222
  225.1 18.2 %all-to-all-done.5 = bf16[32,32,384]{2,1,0:T(8,128)(2,1)S(1)} async-done(((bf16[32,32,384]{2,1,0:T(8,128)(2,1)}), bf16[32,32,384]{2,1,0:T(8,128)(2,1)S(1)}, u32[]{:S(2)}, u32[]{:S(2)}) %all-to-all-start.5) | async-done | bytes 786464 | tf_op jit(solution)/shard_map/backward/all_to_all | solution.py:222
  (97 shorter events, 28.8 us)
Async XLA Ops:
  7.2 145.7 %all-gather.2.cloned.1.call-start = ((), (), s32[]{:S(2)}) async-start(), calls=%async_computation.6 | async-start | bytes 4792320 | tf_op jit(solution)/shard_map/weights/all_gather | solution.py:124
  10.8 25.2 %all-to-all-start = ((s32[64,3,128]{2,1,0:T(4,128)}), s32[64,3,128]{2,1,0:T(4,128)S(1)}, u32[]{:S(2)}, u32[]{:S(2)}) async-start(s32[64,3,128]{2,1,0:T(4,128)} %broadcast_in_dim.21), calls=%async_computation | async-start | bytes 262144 | tf_op jit(solution)/shard_map/ids/all_to_all | solution.py:23
  25.6 1.6 copy-start.2
  33.1 2.0 copy-start
  36.0 0.6 copy-start.4
  36.6 2.2 copy-start.1
  113.3 6.4 %copy-start.15 = (s32[2,2]{1,0:T(2,128)S(1)}, s32[2,2]{1,0:T(2,128)}, u32[]{:S(2)}) copy-start(s32[2,2]{1,0:T(2,128)} %param.9) | copy-start | bytes 52
  115.0 33.9 %all-to-all-start.2 = ((bf16[8,256,256]{2,1,0:T(8,128)(2,1)}), bf16[8,256,256]{2,1,0:T(8,128)(2,1)S(1)}, u32[]{:S(2)}, u32[]{:S(2)}) async-start(bf16[8,256,256]{2,1,0:T(8,128)(2,1)} %broadcast_in_dim.25), calls=%async_computation.2 | async-start | bytes 2097152 | tf_op jit(solution)/shard_map/embed_exchange/all_to_all | solution.py:23
  119.8 30.7 %copy-start.9 = (s32[4]{0:T(128)}, s32[4]{0:T(128)S(1)}, u32[]{:S(2)}) copy-start(s32[4]{0:T(128)S(1)} %lt.57) | copy-start | bytes 52
  150.5 2.4 copy-start.8
  152.9 3.4 %copy-start.3 = (f32[2048,256]{1,0:T(8,128)S(1)}, f32[2048,256]{1,0:T(8,128)}, u32[]{:S(2)}) copy-start(f32[2048,256]{1,0:T(8,128)} %reshape.170) | copy-start | bytes 6291460
  158.8 7.0 %copy-start.10 = (s32[4]{0:T(128)S(1)}, s32[4]{0:T(128)}, u32[]{:S(2)}) copy-start(s32[4]{0:T(128)} %copy-done.9) | copy-start | bytes 52
  161.5 15.9 %all-to-all-start.3 = ((f32[8,4,2048]{2,1,0:T(4,128)}), f32[8,4,2048]{2,1,0:T(4,128)}, u32[]{:S(2)}, u32[]{:S(2)}) async-start(f32[8,4,2048]{2,1,0:T(4,128)} %broadcast_in_dim.26), calls=%async_computation.3 | async-start | bytes 524288 | tf_op jit(solution)/shard_map/pool/all_to_all | solution.py:23
  175.0 12.3 %copy-start.11 = (s32[4]{0:T(128)S(1)}, s32[4]{0:T(128)}, u32[]{:S(2)}) copy-start(s32[4]{0:T(128)} %copy-done.9) | copy-start | bytes 52
  179.4 2.3 copy-start.5
  181.8 22.8 %all-to-all-start.4 = ((bf16[64,4,1024]{2,1,0:T(4,128)(2,1)}), bf16[64,4,1024]{2,1,0:T(4,128)(2,1)S(1)}, u32[]{:S(2)}, u32[]{:S(2)}) async-start(bf16[64,4,1024]{2,1,0:T(4,128)(2,1)} %bitcast.9), calls=%async_computation.4 | async-start | bytes 1048576 | tf_op jit(solution)/shard_map/scores/all_to_all | solution.py:179
  204.6 3.8 %collective-permute-start = (bf16[64,4,1024]{2,1,0:T(4,128)(2,1)S(1)}, bf16[64,4,1024]{2,1,0:T(4,128)(2,1)S(1)}, u32[]{:S(2)}, u32[]{:S(2)}) collective-permute-start(bf16[64,4,1024]{2,1,0:T(4,128)(2,1)S(1)} %all-to-all-done.4), channel_id=1, source_target_pairs={{0,8},{8,0},{16,24},{24,16},{32,40},{40,32},{48,56},{56,48},{64,72... | collective-permute-start | bytes 1572872 | tf_op jit(solution)/shard_map/scores/ppermute | solution.py:182
  208.4 2.8 %copy-start.12 = (f32[4]{0:T(128)S(1)}, f32[4]{0:T(128)}, u32[]{:S(2)}) copy-start(f32[4]{0:T(128)} %convert_element_type.95) | copy-start | bytes 52
  208.4 2.8 %copy-start.14 = (f32[4]{0:T(128)S(1)}, f32[4]{0:T(128)}, u32[]{:S(2)}) copy-start(f32[4]{0:T(128)} %copy-done.13) | copy-start | bytes 52
  208.4 0.8 copy-start.7
  208.4 2.6 %copy-start.6 = (f32[4,2048]{1,0:T(4,128)S(1)}, f32[4,2048]{1,0:T(4,128)}, u32[]{:S(2)}) copy-start(f32[4,2048]{1,0:T(4,128)} %copy-done.5) | copy-start | bytes 98308
  208.4 2.8 %copy-start.16 = (f32[4]{0:T(128)S(1)}, f32[4]{0:T(128)}, u32[]{:S(2)}) copy-start(f32[4]{0:T(128)} %get-tuple-element.16) | copy-start | bytes 52
  213.5 4.2 %collective-permute-start.1 = (bf16[1024,384]{1,0:T(8,128)(2,1)S(1)}, bf16[1024,384]{1,0:T(8,128)(2,1)S(1)}, u32[]{:S(2)}, u32[]{:S(2)}) collective-permute-start(bf16[1024,384]{1,0:T(8,128)(2,1)S(1)} %convolution_convert_fusion), channel_id=1, source_target_pairs={{0,8},{8,0},{16,24},{24,16},{32,40},{40,32},{48,56},{56,48},{64,72... | collective-permute-start | bytes 2359304 | tf_op jit(solution)/shard_map/backward/ppermute | solution.py:219
  219.0 24.3 %all-to-all-start.5 = ((bf16[32,32,384]{2,1,0:T(8,128)(2,1)}), bf16[32,32,384]{2,1,0:T(8,128)(2,1)S(1)}, u32[]{:S(2)}, u32[]{:S(2)}) async-start(bf16[32,32,384]{2,1,0:T(8,128)(2,1)} %bitcast.13), calls=%async_computation.5 | async-start | bytes 1572864 | tf_op jit(solution)/shard_map/backward/all_to_all | solution.py:222
  (1 other events, 0.6 us)
Sparse Core Ops, SparseCore 0:
  11.3 111.0 all-gather.1

commit v3 on v2

--- a/solution.py
+++ b/solution.py
@@ -23,6 +23,28 @@
     return lax.all_to_all(copies, axis, 0, 0, tiled=True)
 
 
+def ids_kernel(pos_ref, ids_ref, out_ref):
+    sides, pair_dev, seq_len = ids_ref.shape
+    ids = jnp.concatenate(
+        [ids_ref[side, pl.ds(pair, 1), :] for side in range(sides) for pair in range(pair_dev)], axis=1
+    )
+    lane = lax.broadcasted_iota(jnp.int32, (1, lanes), 1)
+    marks = jnp.zeros((1, lanes), jnp.int32)
+    for pair in range(pair_dev):
+        marks = jnp.where(lane == pair, pos_ref[pair], marks)
+    rows = [ids[:, start : start + lanes] for start in range(0, ids.shape[1], lanes)] + [marks]
+    out_ref[...] = jnp.broadcast_to(jnp.concatenate(rows, axis=0)[None], out_ref.shape)
+
+
+def spread_ids(token_ids, positives, count):
+    return pl.pallas_call(
+        ids_kernel,
+        out_shape=jax.ShapeDtypeStruct((count, token_ids.size // lanes + 1, lanes), jnp.int32),
+        in_specs=[pl.BlockSpec(memory_space=pltpu.SMEM), pl.BlockSpec(memory_space=pltpu.VMEM)],
+        out_specs=pl.BlockSpec(memory_space=pltpu.VMEM),
+    )(positives, token_ids)
+
+
 def pack_kernel(span, table_ref, rows_ref):
     feats, vocab = table_ref.shape
     slots = lanes // feats
@@ -36,7 +58,7 @@
     def _(step):
         start = pl.multiple_of(step * lanes, lanes)
         stacked = jnp.concatenate([piece(slot, start, lanes) for slot in range(slots)], axis=0)
-        rows_ref[pl.ds(start, lanes), :] = stacked.T
+        rows_ref[pl.ds(start, lanes), 0, :] = stacked.T
 
     for step in range(whole, span // lanes):
         start = step * lanes
@@ -45,26 +67,50 @@
         if left:
             last = jnp.concatenate([piece(slots - 1, start, left), last], axis=1)
         stacked = jnp.concatenate([piece(slot, start, lanes) for slot in range(slots - 1)] + [last], axis=0)
-        rows_ref[start : start + lanes, :] = stacked.T
-
-
-def pick_kernel(row_ref, slot_ref, rows_ref, out_ref, held_ref):
+        rows_ref[start : start + lanes, 0, :] = stacked.T
+
+
+def pick_kernel(chunks, row_ref, slot_ref, rows_ref, out_ref, even_ref, odd_ref, near_ref, sems):
     groups, tokens = row_ref.shape
     feats = out_ref.shape[1]
     slots = lanes // feats
-
-    @pl.loop(0, groups)
-    def _(group):
+    chunk = groups // chunks
+
+    def bring(index):
+        where = pl.ds(index * chunk, chunk)
+        return pltpu.make_async_copy(row_ref.at[where], near_ref.at[where], sems.at[index])
+
+    def read(group, held_ref):
         for token in range(tokens):
-            held_ref[pl.ds(token, 1), :] = rows_ref[pl.ds(row_ref[group, token], 1), :]
+            held_ref[pl.ds(token, 1), :] = rows_ref[near_ref[group, token]]
+
+    def turn(group, held_ref):
         slot = slot_ref[pl.ds(group, 1), :]
         for first in range(0, tokens, lanes):
             turned = held_ref[first : first + lanes, :].T
             mine = slot[:, first : first + lanes]
             total = jnp.zeros((feats, lanes), jnp.float32)
-            for index in range(slots):
-                total += jnp.where(mine == index, turned[index * feats : (index + 1) * feats], 0.0)
+            for part in range(slots):
+                total = jnp.where(mine == part, turned[part * feats : (part + 1) * feats], total)
             out_ref[group, :, first : first + lanes] = total.astype(out_ref.dtype)
+
+    for index in range(chunks):
+        bring(index).start()
+    bring(0).wait()
+    read(0, even_ref)
+
+    @pl.loop(0, groups // 2)
+    def _(step):
+        ahead = step * 2 // chunk + 1
+
+        @pl.when((step * 2 % chunk == 0) & (ahead < chunks))
+        def _():
+            bring(ahead).wait()
+
+        read(step * 2 + 1, odd_ref)
+        turn(step * 2, even_ref)
+        read(jnp.minimum(step * 2 + 2, groups - 1), even_ref)
+        turn(step * 2 + 1, odd_ref)
 
 
 def pack_table(table):
@@ -73,11 +119,11 @@
     span = -(-vocab // (slots * lanes)) * lanes
     return pl.pallas_call(
         functools.partial(pack_kernel, span),
-        out_shape=jax.ShapeDtypeStruct((span, lanes), jnp.float32),
+        out_shape=jax.ShapeDtypeStruct((span, 1, lanes), jnp.float32),
         in_specs=[pl.BlockSpec(memory_space=pltpu.VMEM)],
         out_specs=pl.BlockSpec(memory_space=pltpu.VMEM),
         compiler_params=pltpu.CompilerParams(vmem_limit_bytes=32 << 20),
-        cost_estimate=pl.CostEstimate(flops=0, bytes_accessed=3 * feats * vocab * 2, transcendentals=0),
+        cost_estimate=pl.CostEstimate(flops=0, bytes_accessed=20 << 20, transcendentals=0),
     )(table)
 
 
@@ -85,24 +131,74 @@
     slots = lanes // feats
     span = packed.shape[0]
     groups, tokens = rows.shape
+    chunks = 8 if groups % 16 == 0 else 1
     inside = (rows >= 0) & (rows < slots * span)
     safe = jnp.where(inside, rows, 0)
     slot = safe // span
     row = safe - slot * span
     slot = jnp.where(inside, slot, slots)
     return pl.pallas_call(
-        pick_kernel,
+        functools.partial(pick_kernel, chunks),
         out_shape=jax.ShapeDtypeStruct((groups, feats, tokens), jnp.bfloat16),
-        in_specs=[
-            pl.BlockSpec(memory_space=pltpu.SMEM),
-            pl.BlockSpec(memory_space=pltpu.VMEM),
-            pl.BlockSpec(memory_space=pltpu.VMEM),
+        in_specs=[pl.BlockSpec(memory_space=pltpu.VMEM)] * 3,
+        out_specs=pl.BlockSpec(memory_space=pltpu.VMEM),
+        scratch_shapes=[
+            pltpu.VMEM((tokens, lanes), jnp.float32),
+            pltpu.VMEM((tokens, lanes), jnp.float32),
+            pltpu.SMEM((groups, tokens), jnp.int32),
+            pltpu.SemaphoreType.DMA((chunks,)),
         ],
-        out_specs=pl.BlockSpec(memory_space=pltpu.VMEM),
-        scratch_shapes=[pltpu.VMEM((tokens, lanes), jnp.float32)],
         compiler_params=pltpu.CompilerParams(vmem_limit_bytes=32 << 20),
         cost_estimate=pl.CostEstimate(flops=0, bytes_accessed=30 << 20, transcendentals=0),
     )(row, slot, packed)
+
+
+def gelu(v):
+    return 0.5 * v * (1.0 + jnp.tanh(0.7978845608028654 * (v + 0.044715 * (v * v * v))))
+
+
+def forward_kernel(units, x_ref, gain_ref, mask_ref, weights_ref, normed_ref, act_ref, out_ref, sum_ref):
+    width, tokens = x_ref.shape
+    resid = x_ref[...].astype(jnp.float32)
+    scale = lax.rsqrt(jnp.mean(resid * resid, axis=0, keepdims=True) + 1e-06)
+    normed_ref[...] = (resid * scale * gain_ref[...]).astype(jnp.bfloat16)
+    first = (((0,), (0,)), ((), ()))
+    both = lax.dot_general(
+        normed_ref[...], weights_ref[:, : 2 * units], first, preferred_element_type=jnp.float32
+    )
+    act = gelu(both[:, :units])
+    act_ref[...] = act
+    hidden = (act * both[:, units:]).astype(jnp.bfloat16)
+    mask = mask_ref[...]
+    hidden_sum = jnp.dot(mask, hidden, preferred_element_type=jnp.float32)
+    high = hidden_sum.astype(jnp.bfloat16)
+    low = (hidden_sum - high.astype(jnp.float32)).astype(jnp.bfloat16)
+    last = (((1,), (1,)), ((), ()))
+    down = weights_ref[:, 2 * units :]
+    terms = lax.dot_general(
+        jnp.concatenate([high, low], axis=0), down, last, preferred_element_type=jnp.float32
+    )
+    rows = mask.shape[0]
+    total = terms[:rows] + terms[rows:]
+    out_ref[...] = jnp.broadcast_to(total[: out_ref.shape[1]][None], out_ref.shape)
+    sum_ref[...] = lax.dot_general(mask, x_ref[...], last, preferred_element_type=jnp.float32)[: sum_ref.shape[0]]
+
+
+def forward(embedded, gain, mask, weights, units, count, sentences):
+    width, tokens = embedded.shape
+    return pl.pallas_call(
+        functools.partial(forward_kernel, units),
+        out_shape=[
+            jax.ShapeDtypeStruct((width, tokens), jnp.bfloat16),
+            jax.ShapeDtypeStruct((tokens, units), jnp.float32),
+            jax.ShapeDtypeStruct((count, sentences, width), jnp.float32),
+            jax.ShapeDtypeStruct((sentences, width), jnp.float32),
+        ],
+        in_specs=[pl.BlockSpec(memory_space=pltpu.VMEM)] * 4,
+        out_specs=[pl.BlockSpec(memory_space=pltpu.VMEM)] * 4,
+        compiler_params=pltpu.CompilerParams(vmem_limit_bytes=40 << 20),
+        cost_estimate=pl.CostEstimate(flops=3 * 2 * width * tokens * units, bytes_accessed=10 << 20, transcendentals=tokens * units),
+    )(embedded, gain, mask, weights)
 
 
 def on_device(token_ids, lengths, positives, embed_table, norm_gain, w_gate, w_up, w_down):
@@ -119,16 +215,21 @@
     even_core = lax.axis_index("dp") % 2 == 0
     swap_cores = [(index, index ^ 1) for index in range(dp_count)]
 
+    with jax.named_scope("ids"):
+        spread = spread_ids(token_ids, positives, dp_count)
+        spread, w_gate, w_up, w_down = lax.optimization_barrier((spread, w_gate, w_up, w_down))
+        arrived = lax.all_to_all(spread, "dp", 0, 0, tiled=True)
+        all_ids = arrived[:, : tokens // lanes].reshape(dp_count, tokens)
+        all_pos = arrived[:, tokens // lanes, :pair_dev].reshape(-1)
+
     with jax.named_scope("weights"):
+        def by_part(rows):
+            rows = rows.reshape((dp_count, tensor_count, part) + rows.shape[1:])
+            return jnp.swapaxes(rows, 0, 1).reshape((width,) + rows.shape[3:])
+
         rows = jnp.concatenate([w_gate, w_up, w_down.T], axis=1)
-        weights = lax.all_gather(rows, "dp", axis=0, tiled=True)
-
-    with jax.named_scope("ids"):
-        flat = jnp.concatenate([token_ids.reshape(-1), positives])
-        flat = jnp.pad(flat, (0, -flat.shape[0] % 128)).reshape(-1, 128)
-        arrived = gather_all(flat, "dp").reshape(dp_count, -1)
-        all_ids = arrived[:, :tokens]
-        all_pos = arrived[:, tokens : tokens + pair_dev].reshape(-1)
+        weights = by_part(lax.all_gather(rows, "dp", axis=0, tiled=True))
+        gain = by_part(norm_gain[:, None])
 
     with jax.named_scope("lookup"):
         local_ids = all_ids - lax.axis_index("tensor") * vocab_block
@@ -141,34 +242,23 @@
         blocks = blocks.reshape(dp_count, tensor_count, part, tokens)
         mine = jnp.sum(blocks.astype(jnp.float32), axis=1).astype(jnp.bfloat16)
         mine = mine.reshape(dp_count * part, tokens)
-        full = gather_all(mine, "tensor").reshape(tensor_count, dp_count, part, tokens)
-        embedded = full.transpose(1, 0, 2, 3).reshape(width, tokens)
+        embedded = gather_all(mine, "tensor").reshape(width, tokens)
 
     with jax.named_scope("forward"):
-        resid = embedded.astype(jnp.float32)
-        scale = lax.rsqrt(jnp.mean(resid * resid, axis=0, keepdims=True) + 1e-06)
-        normed = (resid * scale * norm_gain[:, None]).astype(jnp.bfloat16)
-        gate_proj = product(weights[:, :units], normed, 0, 0)
-        up_proj = product(weights[:, units : 2 * units], normed, 0, 0)
+        sentences = 2 * pair_dev
+        positions = jnp.arange(seq_len, dtype=jnp.int32)
+        pad_mask = positions[None, :] < lengths.reshape(-1)[:, None]
+        chosen_tokens = jnp.eye(16, sentences, dtype=jnp.bool_)[:, :, None] & pad_mask[None]
+        chosen_tokens = chosen_tokens.reshape(16, tokens).astype(jnp.bfloat16)
+        normed, activated, partial_out, resid_sum = forward(
+            embedded, gain, chosen_tokens, weights, units, tensor_count, sentences
+        )
         down = weights[:, 2 * units :]
-        activated = jax.nn.gelu(gate_proj, approximate=True)
-        hidden = lax.reduce_precision(activated * up_proj, 8, 7)
 
     with jax.named_scope("pool"):
         seq_lens = lengths.reshape(-1).astype(jnp.float32)
-        positions = jnp.arange(seq_len, dtype=jnp.int32)
-        pad_mask = (positions[None, :] < lengths.reshape(-1)[:, None]).astype(jnp.float32)
-        sentences = 2 * pair_dev
-        hidden_sum = jnp.sum(
-            hidden.reshape(units, sentences, seq_len) * pad_mask[None], axis=2
-        )
-        resid_sum = jnp.sum(resid.reshape(width, sentences, seq_len) * pad_mask[None], axis=2)
-        high = lax.reduce_precision(hidden_sum, 8, 7)
-        terms = jnp.concatenate([high, hidden_sum - high], axis=1).astype(jnp.bfloat16)
-        both = product(terms, down, 0, 1)
-        partial_out = both[:sentences] + both[sentences:]
-        out_sum = jnp.sum(gather_all(partial_out, "tensor"), axis=0)
-        pooled = (resid_sum.T + out_sum) / seq_lens[:, None]
+        out_sum = jnp.sum(lax.all_to_all(partial_out, "tensor", 0, 0, tiled=True), axis=0)
+        pooled = (resid_sum + out_sum) / seq_lens[:, None]
         inv_rms = lax.rsqrt(jnp.mean(pooled * pooled, axis=-1, keepdims=True) + 1e-06)
         reps = (pooled * inv_rms).astype(jnp.bfloat16)
 
@@ -209,15 +299,15 @@
             - pooled * inv_rms**3 * jnp.sum(grad_reps * pooled, axis=-1, keepdims=True) / width
         )
         token_grad = (grad_pooled / seq_lens[:, None]).astype(jnp.bfloat16)
-        d_hidden = product(down, token_grad, 0, 1)
-        d_tokens = (d_hidden[:, :, None] * pad_mask[None]).reshape(units, tokens)
+        d_hidden = product(token_grad, down, 1, 0)
+        d_tokens = jnp.where(pad_mask[:, :, None], d_hidden[:, None, :], 0.0).reshape(tokens, units)
         d_up = (d_tokens * activated).astype(jnp.bfloat16)
-        by_core = normed.reshape(dp_count // 2, 2, feats, tokens)
-        own_rows = jnp.where(even_core, by_core[:, 0], by_core[:, 1]).reshape(-1, tokens)
-        other_rows = jnp.where(even_core, by_core[:, 1], by_core[:, 0]).reshape(-1, tokens)
-        sent = product(other_rows, d_up, 1, 1).astype(jnp.bfloat16)
+        by_core = normed.reshape(tensor_count, dp_count // 2, 2, part, tokens)
+        sides = [jnp.where(even_core == side, by_core[:, :, 0], by_core[:, :, 1]) for side in (True, False)]
+        own_rows, other_rows = (jnp.swapaxes(side, 0, 1).reshape(-1, tokens) for side in sides)
+        sent = product(other_rows, d_up, 1, 0).astype(jnp.bfloat16)
         got = lax.ppermute(sent, "dp", swap_cores)
-        partial_grad = (product(own_rows, d_up, 1, 1) + got.astype(jnp.float32)).astype(jnp.bfloat16)
+        partial_grad = (product(own_rows, d_up, 1, 0) + got.astype(jnp.float32)).astype(jnp.bfloat16)
         same_core = [list(range(core, dp_count, 2)) for core in range(2)]
         parts = lax.all_to_all(
             partial_grad.reshape(dp_count // 2, feats, units),

time: 256 us -> 252 us (0.984)
  local copies, waits for them, and re-layouts: 23.4 us -> 41.9 us
  other arithmetic: 15.9 us -> 5.83 us
  waiting for transfers between devices: 63.8 us -> 53.9 us
  matrix products: 13.3 us -> 4.83 us
  starting transfers between devices: 39.3 us -> 44.4 us
    all_to_all x3 -> x1, waiting for transfers between devices: 31.3 us -> 0.01 us  [gather_all(): return lax.all_to_all(copies, axis, 0, 0, tiled=True)]
    reshape x1 -> x7, local copies, waits for them, and re-layouts: 0.76 us -> 24.4 us  [the longest x2 15.1 us: by_part(): rows = rows.reshape((dp_count, tensor_count, part) + rows.shape[1:])]
    all_to_all x0 -> x2, starting transfers between devices: none -> 21.4 us  [the longest x1 14.8 us: on_device(): arrived = lax.all_to_all(spread, 'dp', 0, 0, tiled=True)]
    all_to_all x3 -> x1, starting transfers between devices: 23.8 us -> 4.69 us  [gather_all(): return lax.all_to_all(copies, axis, 0, 0, tiled=True)]
    all_to_all x0 -> x2, waiting for transfers between devices: none -> 12 us  [the longest x1 11.9 us: on_device(): lax.all_to_all(partial_out, 'tensor', 0, 0, tiled=True)]
    dot_general x12 -> x9, matrix products: 13.3 us -> 4.83 us  [product(): lax.dot_general(left, right, (((left_dim,), (right_dim,)), ((), ())), pre...]
    convert_element_type x4 -> x0, local copies, waits for them, and re-layouts: 8.18 us -> none  [on_device(): resid = embedded.astype(jnp.float32)]
    reduce_sum x3 -> x1, other arithmetic: 6.61 us -> 0.05 us  [on_device(): jnp.sum(lax.all_to_all(partial_out, 'tensor', 0, 0, tiled=True), axis=0)]
  transfers between devices with their start and end apart: 8 -> 8, of which waited for: 6 -> 7; matrix products, arithmetic and copies ran while one was open for 10% -> 12% of each run, Pallas kernels for 13% -> 11%
where the time goes in v3:
time: 252 us; the launch traced here: 248 us
  waiting for transfers between devices  53.9 us (21%)
  blocking collectives  49.2 us (20%)
  starting transfers between devices  44.4 us (18%)
  local copies, waits for them, and re-layouts  41.9 us (17%)
  Pallas kernels  31.6 us (13%)
  between operations  16.1 us (6%)
  other arithmetic  5.83 us (2%)
  matrix products  4.83 us (2%)
    all_to_all x1, blocking collectives, on_device(): blocks = lax.all_to_all(blocks, ('dp', 'tensor'), 0, 0, tiled=True)  49.2 us
    pallas_call x1, Pallas kernels, pick_rows(): pl.pallas_call(functools.partial(pick_kernel, chunks), out_shape=jax.Shap...  20.7 us
    all_to_all x1, waiting for transfers between devices, on_device(): lax.all_to_all(partial_grad.reshape(dp_count // 2, feats, units), 'dp', 0...  18.3 us
    all_to_all x1, waiting for transfers between devices, on_device(): lax.all_to_all(halves.reshape(dp_count, 2 * pair_dev, half), 'dp', 0, 0,...  15.4 us
    reshape x2, local copies, waits for them, and re-layouts, by_part(): rows = rows.reshape((dp_count, tensor_count, part) + rows.shape[1:])  15.1 us
    all_to_all x1, starting transfers between devices, on_device(): arrived = lax.all_to_all(spread, 'dp', 0, 0, tiled=True)  14.8 us
    all_to_all x1, waiting for transfers between devices, on_device(): lax.all_to_all(partial_out, 'tensor', 0, 0, tiled=True)  11.9 us
    unnamed x24, local copies, waits for them, and re-layouts  10 us
  transfers between devices with their start and end apart: 8, of which 7 were waited for; matrix products, arithmetic and copies ran while one was open for 12% of the time, Pallas kernels for 11%

profile of v3, /device:TPU:1, one launch (start us, length us, event | category | flops | bytes accessed | tf_op | source)
XLA Modules:
  0.0 247.7 jit_solution(14955741738193961865)
XLA Ops:
  10.1 14.8 %all-to-all-start = ((s32[64,3,128]{2,1,0:T(4,128)}), s32[64,3,128]{2,1,0:T(4,128)S(1)}, u32[]{:S(2)}, u32[]{:S(2)}) async-start(s32[64,3,128]{2,1,0:T(4,128)} %ids.1), calls=%async_computation | async-start | bytes 262144 | tf_op jit(solution)/shard_map/ids/all_to_all | solution.py:221
  26.5 6.6 %lookup.2.rows_ref = f32[7936,1,128]{2,1,0:T(1,128)S(1)} custom-call(bf16[32,31264]{1,0:T(8,128)(2,1)S(1)} %copy-done.3), custom_call_target="tpu_custom_call" | custom-call | bytes 20971520 | tf_op jit(solution)/shard_map/lookup/pallas_call | solution.py:120
  33.1 2.0 copy-done.1
  35.9 2.2 copy-done.2
  38.1 20.7 %lookup.3 = bf16[64,32,256]{2,1,0:T(8,128)(2,1)S(1)} custom-call(s32[64,256]{1,0:T(8,128)S(1)} %get-tuple-element.31.row_ref, s32[64,256]{1,0:T(8,128)S(1)} %get-tuple-element.30.slot_ref, f32[7936,1,128]{2,1,0:T(1,128)S(1)} %copy-done.2), custom_call_target="tpu_custom_call" | custom-call | bytes 31457280 | tf_op jit(solution)/shard_map/lookup/pallas_call | solution.py:140
  59.1 49.2 %all_to_all.30 = bf16[512,4,256]{2,1,0:T(4,128)(2,1)S(1)} all-to-all(bf16[512,4,256]{2,1,0:T(4,128)(2,1)S(1)} %reshape.148), channel_id=1, replica_groups=mesh['dp'=64,'tensor'=8] {'dp','tensor'}, dimensions={0} | all-to-all | bytes 2097152 | tf_op jit(solution)/shard_map/embed_exchange/all_to_all | solution.py:241
  110.0 4.7 %all-to-all-start.2 = ((bf16[8,256,256]{2,1,0:T(8,128)(2,1)}), bf16[8,256,256]{2,1,0:T(8,128)(2,1)S(1)}, u32[]{:S(2)}, u32[]{:S(2)}) async-start(bf16[8,256,256]{2,1,0:T(8,128)(2,1)} %broadcast_in_dim.61), calls=%async_computation.2 | async-start | bytes 2097152 | tf_op jit(solution)/shard_map/embed_exchange/all_to_all | solution.py:23
  116.0 6.1 %all-gather.2.cloned.1.call-done = bf16[2048,1152]{1,0:T(8,128)(2,1)} async-done(((bf16[32,1152]{1,0:T(8,128)(2,1)}), bf16[2048,1152]{1,0:T(8,128)(2,1)}) %all-gather.2.cloned.1.call-update) | async-done | bytes 4718608 | tf_op jit(solution)/shard_map/weights/all_gather | solution.py:231
  122.1 8.9 %reshape.152 = bf16[64,8,4,1152]{3,2,1,0:T(4,128)(2,1)} reshape(bf16[2048,1152]{1,0:T(8,128)(2,1)} %all-gather.2.cloned.1.call-done) | data formatting | bytes 9437184 | tf_op jit(solution)/shard_map/weights/reshape | solution.py:227
  131.0 6.2 %copy.31 = bf16[64,8,4,1152]{3,2,0,1:T(4,128)(2,1)} copy(bf16[64,8,4,1152]{3,2,1,0:T(4,128)(2,1)} %reshape.152) | data formatting | bytes 9437184 | tf_op jit(solution)/shard_map/weights/reshape | solution.py:227
  137.2 8.5 %reshape.153.weights_ref = bf16[2048,1152]{1,0:T(8,128)(2,1)} reshape(bf16[8,64,4,1152]{3,2,1,0:T(4,128)(2,1)} %bitcast.57) | data formatting | bytes 9437184 | tf_op jit(solution)/shard_map/weights/reshape | solution.py:228
  145.7 2.3 copy-done
  148.1 2.9 %forward.1 = (bf16[2048,256]{1,0:T(8,128)(2,1)S(1)}, f32[256,384]{1,0:T(8,128)S(1)}, f32[8,4,2048]{2,1,0:T(4,128)S(1)}, f32[4,2048]{1,0:T(4,128)S(1)}) custom-call(bf16[2048,256]{1,0:T(8,128)(2,1)S(1)} %bitcast.56, f32[2048,1]{1,0:T(8,128)S(1)} %reshape.164.gain_ref, bf16[16,256]{1,0:T(8,128)(2,1)S(1)} %and_convert_fusion.mask_ref, ...), custom_call_target="tpu_custom_call" | custom-call | flops 1207959552 | bytes 10485760 | tf_op jit(solution)/shard_map/forward/pallas_call | solution.py:189
  152.3 6.6 %all-to-all-start.3 = ((f32[8,4,2048]{2,1,0:T(4,128)}), f32[8,4,2048]{2,1,0:T(4,128)S(1)}, u32[]{:S(2)}, u32[]{:S(2)}) async-start(f32[8,4,2048]{2,1,0:T(4,128)} %copy-done.4), calls=%async_computation.3 | async-start | bytes 524288 | tf_op jit(solution)/shard_map/pool/all_to_all | solution.py:260
  158.9 11.9 %all-to-all-done.3 = f32[8,4,2048]{2,1,0:T(4,128)S(1)} async-done(((f32[8,4,2048]{2,1,0:T(4,128)}), f32[8,4,2048]{2,1,0:T(4,128)S(1)}, u32[]{:S(2)}, u32[]{:S(2)}) %all-to-all-start.3) | async-done | bytes 262176 | tf_op jit(solution)/shard_map/pool/all_to_all | solution.py:260
  173.5 8.4 %all-to-all-start.4 = ((bf16[64,4,1024]{2,1,0:T(4,128)(2,1)}), bf16[64,4,1024]{2,1,0:T(4,128)(2,1)S(1)}, u32[]{:S(2)}, u32[]{:S(2)}) async-start(bf16[64,4,1024]{2,1,0:T(4,128)(2,1)} %bitcast.6), calls=%async_computation.4 | async-start | bytes 1048576 | tf_op jit(solution)/shard_map/scores/all_to_all | solution.py:269
  183.8 15.4 %all-to-all-done.4 = bf16[64,4,1024]{2,1,0:T(4,128)(2,1)S(1)} async-done(((bf16[64,4,1024]{2,1,0:T(4,128)(2,1)}), bf16[64,4,1024]{2,1,0:T(4,128)(2,1)S(1)}, u32[]{:S(2)}, u32[]{:S(2)}) %all-to-all-start.4) | async-done | bytes 524320 | tf_op jit(solution)/shard_map/scores/all_to_all | solution.py:269
  199.2 2.2 collective-permute-start
  203.1 1.7 fusion.26
  206.9 1.8 fusion
  209.2 2.2 collective-permute-start.1
  211.6 1.8 collective-permute-done.1
  214.7 5.5 %all-to-all-start.5 = ((bf16[32,32,384]{2,1,0:T(8,128)(2,1)}), bf16[32,32,384]{2,1,0:T(8,128)(2,1)S(1)}, u32[]{:S(2)}, u32[]{:S(2)}) async-start(bf16[32,32,384]{2,1,0:T(8,128)(2,1)} %bitcast.12), calls=%async_computation.5 | async-start | bytes 1572864 | tf_op jit(solution)/shard_map/backward/all_to_all | solution.py:312
  220.7 18.3 %all-to-all-done.5 = bf16[32,32,384]{2,1,0:T(8,128)(2,1)S(1)} async-done(((bf16[32,32,384]{2,1,0:T(8,128)(2,1)}), bf16[32,32,384]{2,1,0:T(8,128)(2,1)S(1)}, u32[]{:S(2)}, u32[]{:S(2)}) %all-to-all-start.5) | async-done | bytes 786464 | tf_op jit(solution)/shard_map/backward/all_to_all | solution.py:312
  (83 shorter events, 21.0 us)
Async XLA Ops:
  7.2 115.0 %all-gather.2.cloned.1.call-start = ((), (), s32[]{:S(2)}) async-start(), calls=%async_computation.6 | async-start | bytes 4792320 | tf_op jit(solution)/shard_map/weights/all_gather | solution.py:231
  10.1 25.2 %all-to-all-start = ((s32[64,3,128]{2,1,0:T(4,128)}), s32[64,3,128]{2,1,0:T(4,128)S(1)}, u32[]{:S(2)}, u32[]{:S(2)}) async-start(s32[64,3,128]{2,1,0:T(4,128)} %ids.1), calls=%async_computation | async-start | bytes 262144 | tf_op jit(solution)/shard_map/ids/all_to_all | solution.py:221
  24.9 1.6 copy-start.3
  33.1 2.0 copy-start.1
  35.3 0.6 copy-start.6
  35.9 2.2 copy-start.2
  108.9 5.8 %copy-start.10 = (s32[2,2]{1,0:T(2,128)S(1)}, s32[2,2]{1,0:T(2,128)}, u32[]{:S(2)}) copy-start(s32[2,2]{1,0:T(2,128)} %param.9) | copy-start | bytes 52
  108.9 6.5 %copy-start.9 = (f32[2048]{0:T(1024)S(1)}, f32[2048]{0:T(1024)}, u32[]{:S(2)}) copy-start(f32[2048]{0:T(1024)} %param.12) | copy-start | bytes 24580
  110.0 35.7 %all-to-all-start.2 = ((bf16[8,256,256]{2,1,0:T(8,128)(2,1)}), bf16[8,256,256]{2,1,0:T(8,128)(2,1)S(1)}, u32[]{:S(2)}, u32[]{:S(2)}) async-start(bf16[8,256,256]{2,1,0:T(8,128)(2,1)} %broadcast_in_dim.61), calls=%async_computation.2 | async-start | bytes 2097152 | tf_op jit(solution)/shard_map/embed_exchange/all_to_all | solution.py:23
  145.7 2.3 copy-start
  150.9 0.7 copy-start.4
  151.6 0.6 copy-start.5
  152.3 18.4 %all-to-all-start.3 = ((f32[8,4,2048]{2,1,0:T(4,128)}), f32[8,4,2048]{2,1,0:T(4,128)S(1)}, u32[]{:S(2)}, u32[]{:S(2)}) async-start(f32[8,4,2048]{2,1,0:T(4,128)} %copy-done.4), calls=%async_computation.3 | async-start | bytes 524288 | tf_op jit(solution)/shard_map/pool/all_to_all | solution.py:260
  171.7 0.6 copy-start.7
  173.5 25.7 %all-to-all-start.4 = ((bf16[64,4,1024]{2,1,0:T(4,128)(2,1)}), bf16[64,4,1024]{2,1,0:T(4,128)(2,1)S(1)}, u32[]{:S(2)}, u32[]{:S(2)}) async-start(bf16[64,4,1024]{2,1,0:T(4,128)(2,1)} %bitcast.6), calls=%async_computation.4 | async-start | bytes 1048576 | tf_op jit(solution)/shard_map/scores/all_to_all | solution.py:269
  199.2 3.9 %collective-permute-start = (bf16[64,4,1024]{2,1,0:T(4,128)(2,1)S(1)}, bf16[64,4,1024]{2,1,0:T(4,128)(2,1)}, u32[]{:S(2)}, u32[]{:S(2)}) collective-permute-start(bf16[64,4,1024]{2,1,0:T(4,128)(2,1)S(1)} %all-to-all-done.4), channel_id=1, source_target_pairs={{0,8},{8,0},{16,24},{24,16},{32,40},{40,32},{48,56},{56,48},{64,72... | collective-permute-start | bytes 1572872 | tf_op jit(solution)/shard_map/scores/ppermute | solution.py:272
  202.8 3.9 %copy-start.8 = (f32[4,2048]{1,0:T(4,128)S(1)}, f32[4,2048]{1,0:T(4,128)}, u32[]{:S(2)}) copy-start(f32[4,2048]{1,0:T(4,128)} %copy-done.7) | copy-start | bytes 98308
  202.8 4.0 %copy-start.11 = (f32[4]{0:T(128)S(1)}, f32[4]{0:T(128)}, u32[]{:S(2)}) copy-start(f32[4]{0:T(128)} %get-tuple-element.34) | copy-start | bytes 52
  209.2 4.2 %collective-permute-start.1 = (bf16[1024,384]{1,0:T(8,128)(2,1)S(1)}, bf16[1024,384]{1,0:T(8,128)(2,1)S(1)}, u32[]{:S(2)}, u32[]{:S(2)}) collective-permute-start(bf16[1024,384]{1,0:T(8,128)(2,1)S(1)} %convolution_convert_fusion), channel_id=1, source_target_pairs={{0,8},{8,0},{16,24},{24,16},{32,40},{40,32},{48,56},{56,48},{64,72... | collective-permute-start | bytes 2359304 | tf_op jit(solution)/shard_map/backward/ppermute | solution.py:309
  214.7 24.3 %all-to-all-start.5 = ((bf16[32,32,384]{2,1,0:T(8,128)(2,1)}), bf16[32,32,384]{2,1,0:T(8,128)(2,1)S(1)}, u32[]{:S(2)}, u32[]{:S(2)}) async-start(bf16[32,32,384]{2,1,0:T(8,128)(2,1)} %bitcast.12), calls=%async_computation.5 | async-start | bytes 1572864 | tf_op jit(solution)/shard_map/backward/all_to_all | solution.py:312
Sparse Core Ops, SparseCore 0:
  11.3 110.7 all-gather.1

commit v4 on v3

--- a/solution.py
+++ b/solution.py
@@ -122,7 +122,7 @@
         out_shape=jax.ShapeDtypeStruct((span, 1, lanes), jnp.float32),
         in_specs=[pl.BlockSpec(memory_space=pltpu.VMEM)],
         out_specs=pl.BlockSpec(memory_space=pltpu.VMEM),
-        compiler_params=pltpu.CompilerParams(vmem_limit_bytes=32 << 20),
+        compiler_params=pltpu.CompilerParams(vmem_limit_bytes=10 << 20),
         cost_estimate=pl.CostEstimate(flops=0, bytes_accessed=20 << 20, transcendentals=0),
     )(table)
 
@@ -148,7 +148,7 @@
             pltpu.SMEM((groups, tokens), jnp.int32),
             pltpu.SemaphoreType.DMA((chunks,)),
         ],
-        compiler_params=pltpu.CompilerParams(vmem_limit_bytes=32 << 20),
+        compiler_params=pltpu.CompilerParams(vmem_limit_bytes=10 << 20),
         cost_estimate=pl.CostEstimate(flops=0, bytes_accessed=30 << 20, transcendentals=0),
     )(row, slot, packed)
 
@@ -157,9 +157,17 @@
     return 0.5 * v * (1.0 + jnp.tanh(0.7978845608028654 * (v + 0.044715 * (v * v * v))))
 
 
-def forward_kernel(units, x_ref, gain_ref, mask_ref, weights_ref, normed_ref, act_ref, out_ref, sum_ref):
-    width, tokens = x_ref.shape
-    resid = x_ref[...].astype(jnp.float32)
+def forward_kernel(
+    units, feats, x_ref, gain_ref, mask_ref, weights_ref, normed_ref, act_ref, out_ref, sum_ref, resid_ref
+):
+    parts, part_rows, tokens = x_ref.shape
+    part = feats // parts
+    for index in range(parts):
+        rows = x_ref[index].astype(jnp.float32)
+        for block in range(part_rows // part):
+            start = block * feats + index * part
+            resid_ref[start : start + part, :] = rows[block * part : (block + 1) * part]
+    resid = resid_ref[...]
     scale = lax.rsqrt(jnp.mean(resid * resid, axis=0, keepdims=True) + 1e-06)
     normed_ref[...] = (resid * scale * gain_ref[...]).astype(jnp.bfloat16)
     first = (((0,), (0,)), ((), ()))
@@ -181,13 +189,16 @@
     rows = mask.shape[0]
     total = terms[:rows] + terms[rows:]
     out_ref[...] = jnp.broadcast_to(total[: out_ref.shape[1]][None], out_ref.shape)
-    sum_ref[...] = lax.dot_general(mask, x_ref[...], last, preferred_element_type=jnp.float32)[: sum_ref.shape[0]]
-
-
-def forward(embedded, gain, mask, weights, units, count, sentences):
-    width, tokens = embedded.shape
+    sum_ref[...] = lax.dot_general(
+        mask, resid.astype(jnp.bfloat16), last, preferred_element_type=jnp.float32
+    )[: sum_ref.shape[0]]
+
+
+def forward(embedded, gain, mask, weights, units, feats, sentences):
+    count, part_rows, tokens = embedded.shape
+    width = count * part_rows
     return pl.pallas_call(
-        functools.partial(forward_kernel, units),
+        functools.partial(forward_kernel, units, feats),
         out_shape=[
             jax.ShapeDtypeStruct((width, tokens), jnp.bfloat16),
             jax.ShapeDtypeStruct((tokens, units), jnp.float32),
@@ -196,7 +207,8 @@
         ],
         in_specs=[pl.BlockSpec(memory_space=pltpu.VMEM)] * 4,
         out_specs=[pl.BlockSpec(memory_space=pltpu.VMEM)] * 4,
-        compiler_params=pltpu.CompilerParams(vmem_limit_bytes=40 << 20),
+        scratch_shapes=[pltpu.VMEM((width, tokens), jnp.float32)],
+        compiler_params=pltpu.CompilerParams(vmem_limit_bytes=20 << 20),
         cost_estimate=pl.CostEstimate(flops=3 * 2 * width * tokens * units, bytes_accessed=10 << 20, transcendentals=tokens * units),
     )(embedded, gain, mask, weights)
 
@@ -223,13 +235,8 @@
         all_pos = arrived[:, tokens // lanes, :pair_dev].reshape(-1)
 
     with jax.named_scope("weights"):
-        def by_part(rows):
-            rows = rows.reshape((dp_count, tensor_count, part) + rows.shape[1:])
-            return jnp.swapaxes(rows, 0, 1).reshape((width,) + rows.shape[3:])
-
         rows = jnp.concatenate([w_gate, w_up, w_down.T], axis=1)
-        weights = by_part(lax.all_gather(rows, "dp", axis=0, tiled=True))
-        gain = by_part(norm_gain[:, None])
+        weights = lax.all_gather(rows, "dp", axis=0, tiled=True)
 
     with jax.named_scope("lookup"):
         local_ids = all_ids - lax.axis_index("tensor") * vocab_block
@@ -242,7 +249,7 @@
         blocks = blocks.reshape(dp_count, tensor_count, part, tokens)
         mine = jnp.sum(blocks.astype(jnp.float32), axis=1).astype(jnp.bfloat16)
         mine = mine.reshape(dp_count * part, tokens)
-        embedded = gather_all(mine, "tensor").reshape(width, tokens)
+        embedded = gather_all(mine, "tensor")
 
     with jax.named_scope("forward"):
         sentences = 2 * pair_dev
@@ -251,7 +258,7 @@
         chosen_tokens = jnp.eye(16, sentences, dtype=jnp.bool_)[:, :, None] & pad_mask[None]
         chosen_tokens = chosen_tokens.reshape(16, tokens).astype(jnp.bfloat16)
         normed, activated, partial_out, resid_sum = forward(
-            embedded, gain, chosen_tokens, weights, units, tensor_count, sentences
+            embedded, norm_gain[:, None], chosen_tokens, weights, units, feats, sentences
         )
         down = weights[:, 2 * units :]
 
@@ -302,9 +309,9 @@
         d_hidden = product(token_grad, down, 1, 0)
         d_tokens = jnp.where(pad_mask[:, :, None], d_hidden[:, None, :], 0.0).reshape(tokens, units)
         d_up = (d_tokens * activated).astype(jnp.bfloat16)
-        by_core = normed.reshape(tensor_count, dp_count // 2, 2, part, tokens)
-        sides = [jnp.where(even_core == side, by_core[:, :, 0], by_core[:, :, 1]) for side in (True, False)]
-        own_rows, other_rows = (jnp.swapaxes(side, 0, 1).reshape(-1, tokens) for side in sides)
+        by_core = normed.reshape(dp_count // 2, 2, feats, tokens)
+        own_rows = jnp.where(even_core, by_core[:, 0], by_core[:, 1]).reshape(-1, tokens)
+        other_rows = jnp.where(even_core, by_core[:, 1], by_core[:, 0]).reshape(-1, tokens)
         sent = product(other_rows, d_up, 1, 0).astype(jnp.bfloat16)
         got = lax.ppermute(sent, "dp", swap_cores)
         partial_grad = (product(own_rows, d_up, 1, 0) + got.astype(jnp.float32)).astype(jnp.bfloat16)

time: 252 us -> 243 us (0.964)
  local copies, waits for them, and re-layouts: 41.9 us -> 16 us
  waiting for transfers between devices: 53.9 us -> 77.5 us
  starting transfers between devices: 44.4 us -> 38.3 us
    all_to_all x1, waiting for transfers between devices: 0.01 us -> 28.1 us  [gather_all(): return lax.all_to_all(copies, axis, 0, 0, tiled=True)]
    reshape x7 -> x0, local copies, waits for them, and re-layouts: 24.4 us -> none  [the longest x2 15.1 us: by_part(): rows = rows.reshape((dp_count, tensor_count, part) + rows.shape[1:])]
    all_gather x1, waiting for transfers between devices: 6.11 us -> 0.01 us  [on_device(): weights = lax.all_gather(rows, 'dp', axis=0, tiled=True)]
    all_to_all x1, starting transfers between devices: 6.59 us -> 3.41 us  [on_device(): lax.all_to_all(partial_out, 'tensor', 0, 0, tiled=True)]
    all_to_all x1, starting transfers between devices: 8.35 us -> 5.34 us  [on_device(): lax.all_to_all(halves.reshape(dp_count, 2 * pair_dev, half), 'dp', 0, 0,...]
    unnamed x24 -> x26, local copies, waits for them, and re-layouts: 10 us -> 10.2 us
  transfers between devices with their start and end apart: 8 -> 8, of which waited for: 7 -> 6; matrix products, arithmetic and copies ran while one was open for 12% -> 2% of each run, Pallas kernels for 11% -> 11%
where the time goes in v4:
time: 243 us; the launch traced here: 240 us
  waiting for transfers between devices  77.5 us (32%)
  blocking collectives  49.2 us (20%)
  starting transfers between devices  38.3 us (16%)
  Pallas kernels  31.8 us (13%)
  local copies, waits for them, and re-layouts  16 us (7%)
  between operations  16 us (7%)
  other arithmetic  5.46 us (2%)
  matrix products  5.45 us (2%)
    all_to_all x1, blocking collectives, on_device(): blocks = lax.all_to_all(blocks, ('dp', 'tensor'), 0, 0, tiled=True)  49.2 us
    all_to_all x1, waiting for transfers between devices, gather_all(): return lax.all_to_all(copies, axis, 0, 0, tiled=True)  28.1 us
    pallas_call x1, Pallas kernels, pick_rows(): pl.pallas_call(functools.partial(pick_kernel, chunks), out_shape=jax.Shap...  20.7 us
    all_to_all x1, waiting for transfers between devices, on_device(): lax.all_to_all(partial_grad.reshape(dp_count // 2, feats, units), 'dp', 0...  19.1 us
    all_to_all x1, waiting for transfers between devices, on_device(): lax.all_to_all(halves.reshape(dp_count, 2 * pair_dev, half), 'dp', 0, 0,...  16.2 us
    all_to_all x1, starting transfers between devices, on_device(): arrived = lax.all_to_all(spread, 'dp', 0, 0, tiled=True)  14.8 us
    all_to_all x1, waiting for transfers between devices, on_device(): lax.all_to_all(partial_out, 'tensor', 0, 0, tiled=True)  12 us
    unnamed x26, local copies, waits for them, and re-layouts  10.2 us
  transfers between devices with their start and end apart: 8, of which 6 were waited for; matrix products, arithmetic and copies ran while one was open for 2% of the time, Pallas kernels for 11%

profile of v4, /device:TPU:1, one launch (start us, length us, event | category | flops | bytes accessed | tf_op | source)
XLA Modules:
  0.0 239.8 jit_solution(13526928843759853272)
XLA Ops:
  7.2 1.4 ids.1
  8.6 1.4 pad_maximum_fusion
  10.1 14.8 %all-to-all-start = ((s32[64,3,128]{2,1,0:T(4,128)}), s32[64,3,128]{2,1,0:T(4,128)S(1)}, u32[]{:S(2)}, u32[]{:S(2)}) async-start(s32[64,3,128]{2,1,0:T(4,128)} %ids.1), calls=%async_computation | async-start | bytes 262144 | tf_op jit(solution)/shard_map/ids/all_to_all | solution.py:233
  24.9 1.6 copy-done.3
  26.5 6.6 %lookup.2.rows_ref = f32[7936,1,128]{2,1,0:T(1,128)S(1)} custom-call(bf16[32,31264]{1,0:T(8,128)(2,1)S(1)} %copy-done.3), custom_call_target="tpu_custom_call" | custom-call | bytes 20971520 | tf_op jit(solution)/shard_map/lookup/pallas_call | solution.py:120
  33.1 2.0 copy-done
  35.9 2.2 copy-done.1
  38.1 20.7 %lookup.3 = bf16[64,32,256]{2,1,0:T(8,128)(2,1)S(1)} custom-call(s32[64,256]{1,0:T(8,128)S(1)} %get-tuple-element.29.row_ref, s32[64,256]{1,0:T(8,128)S(1)} %get-tuple-element.28.slot_ref, f32[7936,1,128]{2,1,0:T(1,128)S(1)} %copy-done.1), custom_call_target="tpu_custom_call" | custom-call | bytes 31457280 | tf_op jit(solution)/shard_map/lookup/pallas_call | solution.py:140
  59.1 49.2 %all_to_all.30 = bf16[512,4,256]{2,1,0:T(4,128)(2,1)S(1)} all-to-all(bf16[512,4,256]{2,1,0:T(4,128)(2,1)S(1)} %reshape.136), channel_id=1, replica_groups=mesh['dp'=64,'tensor'=8] {'dp','tensor'}, dimensions={0} | all-to-all | bytes 2097152 | tf_op jit(solution)/shard_map/embed_exchange/all_to_all | solution.py:248
  110.0 4.7 %all-to-all-start.2 = ((bf16[8,256,256]{2,1,0:T(8,128)(2,1)}), bf16[8,256,256]{2,1,0:T(8,128)(2,1)S(1)}, u32[]{:S(2)}, u32[]{:S(2)}) async-start(bf16[8,256,256]{2,1,0:T(8,128)(2,1)} %broadcast_in_dim.61), calls=%async_computation.2 | async-start | bytes 2097152 | tf_op jit(solution)/shard_map/embed_exchange/all_to_all | solution.py:23
  115.8 28.1 %all-to-all-done.2.x_ref = bf16[8,256,256]{2,1,0:T(8,128)(2,1)S(1)} async-done(((bf16[8,256,256]{2,1,0:T(8,128)(2,1)}), bf16[8,256,256]{2,1,0:T(8,128)(2,1)S(1)}, u32[]{:S(2)}, u32[]{:S(2)}) %all-to-all-start.2) | async-done | bytes 1048608 | tf_op jit(solution)/shard_map/embed_exchange/all_to_all | solution.py:23
  143.9 2.3 copy-done.2
  146.2 3.0 %forward.1 = (bf16[2048,256]{1,0:T(8,128)(2,1)S(1)}, f32[256,384]{1,0:T(8,128)S(1)}, f32[8,4,2048]{2,1,0:T(4,128)S(1)}, f32[4,2048]{1,0:T(4,128)S(1)}) custom-call(bf16[8,256,256]{2,1,0:T(8,128)(2,1)S(1)} %all-to-all-done.2.x_ref, f32[2048,1]{1,0:T(8,128)S(1)} %copy.11.gain_ref, bf16[16,256]{1,0:T(8,128)(2,1)S(1)} %and_convert_fusion.mask_ref, ...), custom_call_target="tpu_custom_call" | custom-call | flops 1207959552 | bytes 10485760 | tf_op jit(solution)/shard_map/forward/pallas_call | solution.py:200
  150.6 3.4 %all-to-all-start.3 = ((f32[8,4,2048]{2,1,0:T(4,128)}), f32[8,4,2048]{2,1,0:T(4,128)S(1)}, u32[]{:S(2)}, u32[]{:S(2)}) async-start(f32[8,4,2048]{2,1,0:T(4,128)} %copy-done.4), calls=%async_computation.3 | async-start | bytes 524288 | tf_op jit(solution)/shard_map/pool/all_to_all | solution.py:267
  154.0 12.0 %all-to-all-done.3 = f32[8,4,2048]{2,1,0:T(4,128)S(1)} async-done(((f32[8,4,2048]{2,1,0:T(4,128)}), f32[8,4,2048]{2,1,0:T(4,128)S(1)}, u32[]{:S(2)}, u32[]{:S(2)}) %all-to-all-start.3) | async-done | bytes 262176 | tf_op jit(solution)/shard_map/pool/all_to_all | solution.py:267
  168.8 5.3 %all-to-all-start.4 = ((bf16[64,4,1024]{2,1,0:T(4,128)(2,1)}), bf16[64,4,1024]{2,1,0:T(4,128)(2,1)S(1)}, u32[]{:S(2)}, u32[]{:S(2)}) async-start(bf16[64,4,1024]{2,1,0:T(4,128)(2,1)} %bitcast.4), calls=%async_computation.4 | async-start | bytes 1048576 | tf_op jit(solution)/shard_map/scores/all_to_all | solution.py:276
  175.3 16.2 %all-to-all-done.4 = bf16[64,4,1024]{2,1,0:T(4,128)(2,1)S(1)} async-done(((bf16[64,4,1024]{2,1,0:T(4,128)(2,1)}), bf16[64,4,1024]{2,1,0:T(4,128)(2,1)S(1)}, u32[]{:S(2)}, u32[]{:S(2)}) %all-to-all-start.4) | async-done | bytes 524320 | tf_op jit(solution)/shard_map/scores/all_to_all | solution.py:276
  191.5 2.4 %collective-permute-start = (bf16[64,4,1024]{2,1,0:T(4,128)(2,1)S(1)}, bf16[64,4,1024]{2,1,0:T(4,128)(2,1)S(1)}, u32[]{:S(2)}, u32[]{:S(2)}) collective-permute-start(bf16[64,4,1024]{2,1,0:T(4,128)(2,1)S(1)} %all-to-all-done.4), channel_id=1, source_target_pairs={{0,8},{8,0},{16,24},{24,16},{32,40},{40,32},{48,56},{56,48},{64,72... | collective-permute-start | bytes 1572872 | tf_op jit(solution)/shard_map/scores/ppermute | solution.py:279
  198.1 1.8 fusion
  200.4 2.1 collective-permute-start.1
  202.5 2.1 collective-permute-done.1
  204.6 1.3 add_convert_fusion
  205.9 5.5 %all-to-all-start.5 = ((bf16[32,32,384]{2,1,0:T(8,128)(2,1)}), bf16[32,32,384]{2,1,0:T(8,128)(2,1)S(1)}, u32[]{:S(2)}, u32[]{:S(2)}) async-start(bf16[32,32,384]{2,1,0:T(8,128)(2,1)} %bitcast.9), calls=%async_computation.5 | async-start | bytes 1572864 | tf_op jit(solution)/shard_map/backward/all_to_all | solution.py:319
  212.0 19.1 %all-to-all-done.5 = bf16[32,32,384]{2,1,0:T(8,128)(2,1)S(1)} async-done(((bf16[32,32,384]{2,1,0:T(8,128)(2,1)}), bf16[32,32,384]{2,1,0:T(8,128)(2,1)S(1)}, u32[]{:S(2)}, u32[]{:S(2)}) %all-to-all-start.5) | async-done | bytes 786464 | tf_op jit(solution)/shard_map/backward/all_to_all | solution.py:319
  (76 shorter events, 14.6 us)
Async XLA Ops:
  7.2 136.7 %all-gather.2.cloned.1.call-start = ((), (), s32[]{:S(2)}) async-start(), calls=%async_computation.6 | async-start | bytes 4792320 | tf_op jit(solution)/shard_map/weights/all_gather | solution.py:239
  10.1 25.2 %all-to-all-start = ((s32[64,3,128]{2,1,0:T(4,128)}), s32[64,3,128]{2,1,0:T(4,128)S(1)}, u32[]{:S(2)}, u32[]{:S(2)}) async-start(s32[64,3,128]{2,1,0:T(4,128)} %ids.1), calls=%async_computation | async-start | bytes 262144 | tf_op jit(solution)/shard_map/ids/all_to_all | solution.py:233
  24.9 1.6 copy-start.3
  33.1 2.0 copy-start
  35.3 0.6 copy-start.6
  35.9 2.2 copy-start.1
  108.9 5.8 %copy-start.11 = (s32[2,2]{1,0:T(2,128)S(1)}, s32[2,2]{1,0:T(2,128)}, u32[]{:S(2)}) copy-start(s32[2,2]{1,0:T(2,128)} %param.9) | copy-start | bytes 52
  108.9 5.8 %copy-start.10 = (f32[2048]{0:T(1024)S(1)}, f32[2048]{0:T(1024)}, u32[]{:S(2)}) copy-start(f32[2048]{0:T(1024)} %param.12) | copy-start | bytes 24580
  110.0 33.8 %all-to-all-start.2 = ((bf16[8,256,256]{2,1,0:T(8,128)(2,1)}), bf16[8,256,256]{2,1,0:T(8,128)(2,1)S(1)}, u32[]{:S(2)}, u32[]{:S(2)}) async-start(bf16[8,256,256]{2,1,0:T(8,128)(2,1)} %broadcast_in_dim.61), calls=%async_computation.2 | async-start | bytes 2097152 | tf_op jit(solution)/shard_map/embed_exchange/all_to_all | solution.py:23
  143.9 2.3 copy-start.2
  149.3 0.7 copy-start.4
  150.0 0.6 copy-start.5
  150.6 15.4 %all-to-all-start.3 = ((f32[8,4,2048]{2,1,0:T(4,128)}), f32[8,4,2048]{2,1,0:T(4,128)S(1)}, u32[]{:S(2)}, u32[]{:S(2)}) async-start(f32[8,4,2048]{2,1,0:T(4,128)} %copy-done.4), calls=%async_computation.3 | async-start | bytes 524288 | tf_op jit(solution)/shard_map/pool/all_to_all | solution.py:267
  167.0 0.6 copy-start.7
  168.8 22.7 %all-to-all-start.4 = ((bf16[64,4,1024]{2,1,0:T(4,128)(2,1)}), bf16[64,4,1024]{2,1,0:T(4,128)(2,1)S(1)}, u32[]{:S(2)}, u32[]{:S(2)}) async-start(bf16[64,4,1024]{2,1,0:T(4,128)(2,1)} %bitcast.4), calls=%async_computation.4 | async-start | bytes 1048576 | tf_op jit(solution)/shard_map/scores/all_to_all | solution.py:276
  191.5 3.9 %collective-permute-start = (bf16[64,4,1024]{2,1,0:T(4,128)(2,1)S(1)}, bf16[64,4,1024]{2,1,0:T(4,128)(2,1)S(1)}, u32[]{:S(2)}, u32[]{:S(2)}) collective-permute-start(bf16[64,4,1024]{2,1,0:T(4,128)(2,1)S(1)} %all-to-all-done.4), channel_id=1, source_target_pairs={{0,8},{8,0},{16,24},{24,16},{32,40},{40,32},{48,56},{56,48},{64,72... | collective-permute-start | bytes 1572872 | tf_op jit(solution)/shard_map/scores/ppermute | solution.py:279
  195.4 0.8 copy-start.9
  195.8 2.2 copy-start.8
  195.8 2.3 copy-start.12
  200.4 4.2 %collective-permute-start.1 = (bf16[1024,384]{1,0:T(8,128)(2,1)S(1)}, bf16[1024,384]{1,0:T(8,128)(2,1)S(1)}, u32[]{:S(2)}, u32[]{:S(2)}) collective-permute-start(bf16[1024,384]{1,0:T(8,128)(2,1)S(1)} %convolution_convert_fusion), channel_id=1, source_target_pairs={{0,8},{8,0},{16,24},{24,16},{32,40},{40,32},{48,56},{56,48},{64,72... | collective-permute-start | bytes 2359304 | tf_op jit(solution)/shard_map/backward/ppermute | solution.py:316
  205.9 25.1 %all-to-all-start.5 = ((bf16[32,32,384]{2,1,0:T(8,128)(2,1)}), bf16[32,32,384]{2,1,0:T(8,128)(2,1)S(1)}, u32[]{:S(2)}, u32[]{:S(2)}) async-start(bf16[32,32,384]{2,1,0:T(8,128)(2,1)} %bitcast.9), calls=%async_computation.5 | async-start | bytes 1572864 | tf_op jit(solution)/shard_map/backward/all_to_all | solution.py:319
Sparse Core Ops, SparseCore 0:
  11.3 110.6 all-gather.1

commit v5 on v4

--- a/solution.py
+++ b/solution.py
@@ -158,8 +158,27 @@
 
 
 def forward_kernel(
-    units, feats, x_ref, gain_ref, mask_ref, weights_ref, normed_ref, act_ref, out_ref, sum_ref, resid_ref
+    units,
+    feats,
+    x_ref,
+    gain_ref,
+    mask_ref,
+    weights_ref,
+    normed_ref,
+    act_ref,
+    out_ref,
+    sum_ref,
+    resid_ref,
+    wide_ref,
+    down_ref,
+    total_ref,
+    pool_ref,
+    sems,
 ):
+    bring_wide = pltpu.make_async_copy(weights_ref.at[:, pl.ds(0, 2 * units)], wide_ref, sems.at[0])
+    bring_down = pltpu.make_async_copy(weights_ref.at[:, pl.ds(2 * units, units)], down_ref, sems.at[1])
+    bring_wide.start()
+    bring_down.start()
     parts, part_rows, tokens = x_ref.shape
     part = feats // parts
     for index in range(parts):
@@ -170,33 +189,43 @@
     resid = resid_ref[...]
     scale = lax.rsqrt(jnp.mean(resid * resid, axis=0, keepdims=True) + 1e-06)
     normed_ref[...] = (resid * scale * gain_ref[...]).astype(jnp.bfloat16)
+    mask = mask_ref[...]
     first = (((0,), (0,)), ((), ()))
-    both = lax.dot_general(
-        normed_ref[...], weights_ref[:, : 2 * units], first, preferred_element_type=jnp.float32
-    )
+    last = (((1,), (1,)), ((), ()))
+    sentences = sum_ref.shape[0]
+    pool_ref[...] = lax.dot_general(
+        mask, resid.astype(jnp.bfloat16), last, preferred_element_type=jnp.float32
+    )[:sentences]
+    keep_sum = pltpu.make_async_copy(pool_ref, sum_ref, sems.at[2])
+    keep_sum.start()
+    bring_wide.wait()
+    both = lax.dot_general(normed_ref[...], wide_ref[...], first, preferred_element_type=jnp.float32)
     act = gelu(both[:, :units])
     act_ref[...] = act
     hidden = (act * both[:, units:]).astype(jnp.bfloat16)
-    mask = mask_ref[...]
     hidden_sum = jnp.dot(mask, hidden, preferred_element_type=jnp.float32)
     high = hidden_sum.astype(jnp.bfloat16)
     low = (hidden_sum - high.astype(jnp.float32)).astype(jnp.bfloat16)
-    last = (((1,), (1,)), ((), ()))
-    down = weights_ref[:, 2 * units :]
+    bring_down.wait()
     terms = lax.dot_general(
-        jnp.concatenate([high, low], axis=0), down, last, preferred_element_type=jnp.float32
+        jnp.concatenate([high, low], axis=0), down_ref[...], last, preferred_element_type=jnp.float32
     )
     rows = mask.shape[0]
-    total = terms[:rows] + terms[rows:]
-    out_ref[...] = jnp.broadcast_to(total[: out_ref.shape[1]][None], out_ref.shape)
-    sum_ref[...] = lax.dot_general(
-        mask, resid.astype(jnp.bfloat16), last, preferred_element_type=jnp.float32
-    )[: sum_ref.shape[0]]
+    total_ref[...] = (terms[:rows] + terms[rows:])[:sentences]
+    copies = [
+        pltpu.make_async_copy(total_ref, out_ref.at[index], sems.at[3 + index]) for index in range(parts)
+    ]
+    for copy in copies:
+        copy.start()
+    for copy in copies:
+        copy.wait()
+    keep_sum.wait()
 
 
 def forward(embedded, gain, mask, weights, units, feats, sentences):
     count, part_rows, tokens = embedded.shape
     width = count * part_rows
+    vmem, here = pl.BlockSpec(memory_space=pltpu.VMEM), pl.BlockSpec(memory_space=pl.ANY)
     return pl.pallas_call(
         functools.partial(forward_kernel, units, feats),
         out_shape=[
@@ -205,11 +234,20 @@
             jax.ShapeDtypeStruct((count, sentences, width), jnp.float32),
             jax.ShapeDtypeStruct((sentences, width), jnp.float32),
         ],
-        in_specs=[pl.BlockSpec(memory_space=pltpu.VMEM)] * 4,
-        out_specs=[pl.BlockSpec(memory_space=pltpu.VMEM)] * 4,
-        scratch_shapes=[pltpu.VMEM((width, tokens), jnp.float32)],
-        compiler_params=pltpu.CompilerParams(vmem_limit_bytes=20 << 20),
-        cost_estimate=pl.CostEstimate(flops=3 * 2 * width * tokens * units, bytes_accessed=10 << 20, transcendentals=tokens * units),
+        in_specs=[vmem, vmem, vmem, here],
+        out_specs=[vmem, vmem, here, here],
+        scratch_shapes=[
+            pltpu.VMEM((width, tokens), jnp.float32),
+            pltpu.VMEM((width, 2 * units), jnp.bfloat16),
+            pltpu.VMEM((width, units), jnp.bfloat16),
+            pltpu.VMEM((sentences, width), jnp.float32),
+            pltpu.VMEM((sentences, width), jnp.float32),
+            pltpu.SemaphoreType.DMA((3 + count,)),
+        ],
+        compiler_params=pltpu.CompilerParams(vmem_limit_bytes=24 << 20),
+        cost_estimate=pl.CostEstimate(
+            flops=6 * width * tokens * units, bytes_accessed=10 << 20, transcendentals=tokens * units
+        ),
     )(embedded, gain, mask, weights)
 
 

time: 243 us -> 244 us (level)
  no operation moved by 1% of the time
where the time goes in v5:
time: 244 us; the launch traced here: 241 us
  waiting for transfers between devices  77.6 us (32%)
  blocking collectives  49.2 us (20%)
  starting transfers between devices  38.3 us (16%)
  Pallas kernels  32.6 us (13%)
  local copies, waits for them, and re-layouts  16 us (7%)
  between operations  16 us (7%)
  other arithmetic  5.46 us (2%)
  matrix products  5.44 us (2%)
    all_to_all x1, blocking collectives, on_device(): blocks = lax.all_to_all(blocks, ('dp', 'tensor'), 0, 0, tiled=True)  49.2 us
    all_to_all x1, waiting for transfers between devices, gather_all(): return lax.all_to_all(copies, axis, 0, 0, tiled=True)  28.1 us
    pallas_call x1, Pallas kernels, pick_rows(): pl.pallas_call(functools.partial(pick_kernel, chunks), out_shape=jax.Shap...  20.7 us
    all_to_all x1, waiting for transfers between devices, on_device(): lax.all_to_all(partial_grad.reshape(dp_count // 2, feats, units), 'dp', 0...  19.1 us
    all_to_all x1, waiting for transfers between devices, on_device(): lax.all_to_all(halves.reshape(dp_count, 2 * pair_dev, half), 'dp', 0, 0,...  16.2 us
    all_to_all x1, starting transfers between devices, on_device(): arrived = lax.all_to_all(spread, 'dp', 0, 0, tiled=True)  14.8 us
    all_to_all x1, waiting for transfers between devices, on_device(): lax.all_to_all(partial_out, 'tensor', 0, 0, tiled=True)  12 us
    unnamed x26, local copies, waits for them, and re-layouts  10.2 us
  transfers between devices with their start and end apart: 8, of which 6 were waited for; matrix products, arithmetic and copies ran while one was open for 2% of the time, Pallas kernels for 11%

profile of v5, /device:TPU:1, one launch (start us, length us, event | category | flops | bytes accessed | tf_op | source)
XLA Modules:
  0.0 240.6 jit_solution(16719968758921802452)
XLA Ops:
  7.2 1.4 ids.1
  8.6 1.4 pad_maximum_fusion
  10.1 14.8 %all-to-all-start = ((s32[64,3,128]{2,1,0:T(4,128)}), s32[64,3,128]{2,1,0:T(4,128)S(1)}, u32[]{:S(2)}, u32[]{:S(2)}) async-start(s32[64,3,128]{2,1,0:T(4,128)} %ids.1), calls=%async_computation | async-start | bytes 262144 | tf_op jit(solution)/shard_map/ids/all_to_all | solution.py:271
  24.9 1.6 copy-done.3
  26.5 6.6 %lookup.2.rows_ref = f32[7936,1,128]{2,1,0:T(1,128)S(1)} custom-call(bf16[32,31264]{1,0:T(8,128)(2,1)S(1)} %copy-done.3), custom_call_target="tpu_custom_call" | custom-call | bytes 20971520 | tf_op jit(solution)/shard_map/lookup/pallas_call | solution.py:120
  33.1 2.0 copy-done
  35.9 2.2 copy-done.1
  38.1 20.7 %lookup.3 = bf16[64,32,256]{2,1,0:T(8,128)(2,1)S(1)} custom-call(s32[64,256]{1,0:T(8,128)S(1)} %get-tuple-element.29.row_ref, s32[64,256]{1,0:T(8,128)S(1)} %get-tuple-element.28.slot_ref, f32[7936,1,128]{2,1,0:T(1,128)S(1)} %copy-done.1), custom_call_target="tpu_custom_call" | custom-call | bytes 31457280 | tf_op jit(solution)/shard_map/lookup/pallas_call | solution.py:140
  59.1 49.2 %all_to_all.30 = bf16[512,4,256]{2,1,0:T(4,128)(2,1)S(1)} all-to-all(bf16[512,4,256]{2,1,0:T(4,128)(2,1)S(1)} %reshape.136), channel_id=1, replica_groups=mesh['dp'=64,'tensor'=8] {'dp','tensor'}, dimensions={0} | all-to-all | bytes 2097152 | tf_op jit(solution)/shard_map/embed_exchange/all_to_all | solution.py:286
  110.0 4.7 %all-to-all-start.2 = ((bf16[8,256,256]{2,1,0:T(8,128)(2,1)}), bf16[8,256,256]{2,1,0:T(8,128)(2,1)S(1)}, u32[]{:S(2)}, u32[]{:S(2)}) async-start(bf16[8,256,256]{2,1,0:T(8,128)(2,1)} %broadcast_in_dim.61), calls=%async_computation.2 | async-start | bytes 2097152 | tf_op jit(solution)/shard_map/embed_exchange/all_to_all | solution.py:23
  115.8 28.1 %all-to-all-done.2.x_ref = bf16[8,256,256]{2,1,0:T(8,128)(2,1)S(1)} async-done(((bf16[8,256,256]{2,1,0:T(8,128)(2,1)}), bf16[8,256,256]{2,1,0:T(8,128)(2,1)S(1)}, u32[]{:S(2)}, u32[]{:S(2)}) %all-to-all-start.2) | async-done | bytes 1048608 | tf_op jit(solution)/shard_map/embed_exchange/all_to_all | solution.py:23
  143.9 2.3 copy-done.2
  146.3 3.8 %forward.1 = (bf16[2048,256]{1,0:T(8,128)(2,1)S(1)}, f32[256,384]{1,0:T(8,128)S(1)}, f32[8,4,2048]{2,1,0:T(4,128)S(1)}, f32[4,2048]{1,0:T(4,128)S(1)}) custom-call(bf16[8,256,256]{2,1,0:T(8,128)(2,1)S(1)} %all-to-all-done.2.x_ref, f32[2048,1]{1,0:T(8,128)S(1)} %copy.11.gain_ref, bf16[16,256]{1,0:T(8,128)(2,1)S(1)} %and_convert_fusion.mask_ref, ...), custom_call_target="tpu_custom_call" | custom-call | flops 1207959552 | bytes 10485760 | tf_op jit(solution)/shard_map/forward/pallas_call | solution.py:229
  151.4 3.4 %all-to-all-start.3 = ((f32[8,4,2048]{2,1,0:T(4,128)}), f32[8,4,2048]{2,1,0:T(4,128)S(1)}, u32[]{:S(2)}, u32[]{:S(2)}) async-start(f32[8,4,2048]{2,1,0:T(4,128)} %copy-done.4), calls=%async_computation.3 | async-start | bytes 524288 | tf_op jit(solution)/shard_map/pool/all_to_all | solution.py:305
  154.8 12.0 %all-to-all-done.3 = f32[8,4,2048]{2,1,0:T(4,128)S(1)} async-done(((f32[8,4,2048]{2,1,0:T(4,128)}), f32[8,4,2048]{2,1,0:T(4,128)S(1)}, u32[]{:S(2)}, u32[]{:S(2)}) %all-to-all-start.3) | async-done | bytes 262176 | tf_op jit(solution)/shard_map/pool/all_to_all | solution.py:305
  169.6 5.3 %all-to-all-start.4 = ((bf16[64,4,1024]{2,1,0:T(4,128)(2,1)}), bf16[64,4,1024]{2,1,0:T(4,128)(2,1)S(1)}, u32[]{:S(2)}, u32[]{:S(2)}) async-start(bf16[64,4,1024]{2,1,0:T(4,128)(2,1)} %bitcast.4), calls=%async_computation.4 | async-start | bytes 1048576 | tf_op jit(solution)/shard_map/scores/all_to_all | solution.py:314
  176.1 16.2 %all-to-all-done.4 = bf16[64,4,1024]{2,1,0:T(4,128)(2,1)S(1)} async-done(((bf16[64,4,1024]{2,1,0:T(4,128)(2,1)}), bf16[64,4,1024]{2,1,0:T(4,128)(2,1)S(1)}, u32[]{:S(2)}, u32[]{:S(2)}) %all-to-all-start.4) | async-done | bytes 524320 | tf_op jit(solution)/shard_map/scores/all_to_all | solution.py:314
  192.2 2.4 collective-permute-start
  198.9 1.8 fusion
  201.2 2.1 collective-permute-start.1
  203.3 2.1 collective-permute-done.1
  205.4 1.3 add_convert_fusion
  206.7 5.5 %all-to-all-start.5 = ((bf16[32,32,384]{2,1,0:T(8,128)(2,1)}), bf16[32,32,384]{2,1,0:T(8,128)(2,1)S(1)}, u32[]{:S(2)}, u32[]{:S(2)}) async-start(bf16[32,32,384]{2,1,0:T(8,128)(2,1)} %bitcast.9), calls=%async_computation.5 | async-start | bytes 1572864 | tf_op jit(solution)/shard_map/backward/all_to_all | solution.py:357
  212.8 19.1 %all-to-all-done.5 = bf16[32,32,384]{2,1,0:T(8,128)(2,1)S(1)} async-done(((bf16[32,32,384]{2,1,0:T(8,128)(2,1)}), bf16[32,32,384]{2,1,0:T(8,128)(2,1)S(1)}, u32[]{:S(2)}, u32[]{:S(2)}) %all-to-all-start.5) | async-done | bytes 786464 | tf_op jit(solution)/shard_map/backward/all_to_all | solution.py:357
  (76 shorter events, 14.6 us)
Async XLA Ops:
  7.2 136.8 %all-gather.2.cloned.1.call-start = ((), (), s32[]{:S(2)}) async-start(), calls=%async_computation.6 | async-start | bytes 4792320 | tf_op jit(solution)/shard_map/weights/all_gather | solution.py:277
  10.1 25.2 %all-to-all-start = ((s32[64,3,128]{2,1,0:T(4,128)}), s32[64,3,128]{2,1,0:T(4,128)S(1)}, u32[]{:S(2)}, u32[]{:S(2)}) async-start(s32[64,3,128]{2,1,0:T(4,128)} %ids.1), calls=%async_computation | async-start | bytes 262144 | tf_op jit(solution)/shard_map/ids/all_to_all | solution.py:271
  24.9 1.6 copy-start.3
  33.1 2.0 copy-start
  35.3 0.6 copy-start.6
  35.9 2.2 copy-start.1
  108.9 5.8 %copy-start.11 = (s32[2,2]{1,0:T(2,128)S(1)}, s32[2,2]{1,0:T(2,128)}, u32[]{:S(2)}) copy-start(s32[2,2]{1,0:T(2,128)} %param.9) | copy-start | bytes 52
  108.9 5.9 %copy-start.10 = (f32[2048]{0:T(1024)S(1)}, f32[2048]{0:T(1024)}, u32[]{:S(2)}) copy-start(f32[2048]{0:T(1024)} %param.12) | copy-start | bytes 24580
  110.0 33.9 %all-to-all-start.2 = ((bf16[8,256,256]{2,1,0:T(8,128)(2,1)}), bf16[8,256,256]{2,1,0:T(8,128)(2,1)S(1)}, u32[]{:S(2)}, u32[]{:S(2)}) async-start(bf16[8,256,256]{2,1,0:T(8,128)(2,1)} %broadcast_in_dim.61), calls=%async_computation.2 | async-start | bytes 2097152 | tf_op jit(solution)/shard_map/embed_exchange/all_to_all | solution.py:23
  143.9 2.3 copy-start.2
  150.1 0.7 copy-start.4
  150.8 0.6 copy-start.5
  151.4 15.4 %all-to-all-start.3 = ((f32[8,4,2048]{2,1,0:T(4,128)}), f32[8,4,2048]{2,1,0:T(4,128)S(1)}, u32[]{:S(2)}, u32[]{:S(2)}) async-start(f32[8,4,2048]{2,1,0:T(4,128)} %copy-done.4), calls=%async_computation.3 | async-start | bytes 524288 | tf_op jit(solution)/shard_map/pool/all_to_all | solution.py:305
  167.8 0.6 copy-start.7
  169.6 22.6 %all-to-all-start.4 = ((bf16[64,4,1024]{2,1,0:T(4,128)(2,1)}), bf16[64,4,1024]{2,1,0:T(4,128)(2,1)S(1)}, u32[]{:S(2)}, u32[]{:S(2)}) async-start(bf16[64,4,1024]{2,1,0:T(4,128)(2,1)} %bitcast.4), calls=%async_computation.4 | async-start | bytes 1048576 | tf_op jit(solution)/shard_map/scores/all_to_all | solution.py:314
  192.2 3.9 %collective-permute-start = (bf16[64,4,1024]{2,1,0:T(4,128)(2,1)S(1)}, bf16[64,4,1024]{2,1,0:T(4,128)(2,1)S(1)}, u32[]{:S(2)}, u32[]{:S(2)}) collective-permute-start(bf16[64,4,1024]{2,1,0:T(4,128)(2,1)S(1)} %all-to-all-done.4), channel_id=1, source_target_pairs={{0,8},{8,0},{16,24},{24,16},{32,40},{40,32},{48,56},{56,48},{64,72... | collective-permute-start | bytes 1572872 | tf_op jit(solution)/shard_map/scores/ppermute | solution.py:317
  196.2 0.8 copy-start.9
  196.5 2.2 copy-start.8
  196.5 2.3 copy-start.12
  201.2 4.2 %collective-permute-start.1 = (bf16[1024,384]{1,0:T(8,128)(2,1)S(1)}, bf16[1024,384]{1,0:T(8,128)(2,1)S(1)}, u32[]{:S(2)}, u32[]{:S(2)}) collective-permute-start(bf16[1024,384]{1,0:T(8,128)(2,1)S(1)} %convolution_convert_fusion), channel_id=1, source_target_pairs={{0,8},{8,0},{16,24},{24,16},{32,40},{40,32},{48,56},{56,48},{64,72... | collective-permute-start | bytes 2359304 | tf_op jit(solution)/shard_map/backward/ppermute | solution.py:354
  206.7 25.2 %all-to-all-start.5 = ((bf16[32,32,384]{2,1,0:T(8,128)(2,1)}), bf16[32,32,384]{2,1,0:T(8,128)(2,1)S(1)}, u32[]{:S(2)}, u32[]{:S(2)}) async-start(bf16[32,32,384]{2,1,0:T(8,128)(2,1)} %bitcast.9), calls=%async_computation.5 | async-start | bytes 1572864 | tf_op jit(solution)/shard_map/backward/all_to_all | solution.py:357
Sparse Core Ops, SparseCore 0:
  11.3 110.7 all-gather.1

commit v6 on v5

--- a/solution.py
+++ b/solution.py
@@ -267,8 +267,8 @@
 
     with jax.named_scope("ids"):
         spread = spread_ids(token_ids, positives, dp_count)
-        spread, w_gate, w_up, w_down = lax.optimization_barrier((spread, w_gate, w_up, w_down))
         arrived = lax.all_to_all(spread, "dp", 0, 0, tiled=True)
+        arrived, w_gate, w_up, w_down = lax.optimization_barrier((arrived, w_gate, w_up, w_down))
         all_ids = arrived[:, : tokens // lanes].reshape(dp_count, tokens)
         all_pos = arrived[:, tokens // lanes, :pair_dev].reshape(-1)
 

time: 244 us -> 248 us (1.016)
  blocking collectives: 49.2 us -> 69 us
  starting transfers between devices: 38.3 us -> 23.1 us
    all_to_all x0 -> x1, blocking collectives: none -> 25.2 us  [on_device(): arrived = lax.all_to_all(spread, 'dp', 0, 0, tiled=True)]
    all_to_all x1 -> x0, starting transfers between devices: 14.8 us -> none  [on_device(): arrived = lax.all_to_all(spread, 'dp', 0, 0, tiled=True)]
    all_to_all x1, blocking collectives: 49.2 us -> 43.8 us  [on_device(): blocks = lax.all_to_all(blocks, ('dp', 'tensor'), 0, 0, tiled=True)]
  transfers between devices with their start and end apart: 8 -> 7, of which waited for: 6 -> 5; matrix products, arithmetic and copies ran while one was open for 2% -> 2% of each run, Pallas kernels for 11% -> 11%
where the time goes in v6:
time: 248 us; the launch traced here: 245 us
  waiting for transfers between devices  77.3 us (31%)
  blocking collectives  69 us (28%)
  Pallas kernels  32.6 us (13%)
  starting transfers between devices  23.1 us (9%)
  between operations  16.2 us (7%)
  local copies, waits for them, and re-layouts  15.5 us (6%)
  other arithmetic  5.59 us (2%)
  matrix products  5.45 us (2%)
    all_to_all x1, blocking collectives, on_device(): blocks = lax.all_to_all(blocks, ('dp', 'tensor'), 0, 0, tiled=True)  43.8 us
    all_to_all x1, waiting for transfers between devices, gather_all(): return lax.all_to_all(copies, axis, 0, 0, tiled=True)  28.1 us
    all_to_all x1, blocking collectives, on_device(): arrived = lax.all_to_all(spread, 'dp', 0, 0, tiled=True)  25.2 us
    pallas_call x1, Pallas kernels, pick_rows(): pl.pallas_call(functools.partial(pick_kernel, chunks), out_shape=jax.Shap...  20.7 us
    all_to_all x1, waiting for transfers between devices, on_device(): lax.all_to_all(partial_grad.reshape(dp_count // 2, feats, units), 'dp', 0...  18.9 us
    all_to_all x1, waiting for transfers between devices, on_device(): lax.all_to_all(halves.reshape(dp_count, 2 * pair_dev, half), 'dp', 0, 0,...  16.2 us
    all_to_all x1, waiting for transfers between devices, on_device(): lax.all_to_all(partial_out, 'tensor', 0, 0, tiled=True)  12 us
    unnamed x26, local copies, waits for them, and re-layouts  9.74 us
  transfers between devices with their start and end apart: 7, of which 5 were waited for; matrix products, arithmetic and copies ran while one was open for 2% of the time, Pallas kernels for 11%

profile of v6, /device:TPU:1, one launch (start us, length us, event | category | flops | bytes accessed | tf_op | source)
XLA Modules:
  0.0 244.8 jit_solution(4039321687985068252)
XLA Ops:
  7.2 1.4 ids.1
  8.6 25.2 %all_to_all.30 = s32[64,3,128]{2,1,0:T(4,128)S(1)} all-to-all(s32[64,3,128]{2,1,0:T(4,128)} %ids.1), channel_id=1, replica_groups=mesh['dp'=64,'tensor'=8] {'dp'}, dimensions={0} | all-to-all | bytes 196608 | tf_op jit(solution)/shard_map/ids/all_to_all | solution.py:270
  33.8 1.5 pad_maximum_fusion
  35.3 1.6 copy-done.3
  36.9 6.6 %lookup.2.rows_ref = f32[7936,1,128]{2,1,0:T(1,128)S(1)} custom-call(bf16[32,31264]{1,0:T(8,128)(2,1)S(1)} %copy-done.3), custom_call_target="tpu_custom_call" | custom-call | bytes 20971520 | tf_op jit(solution)/shard_map/lookup/pallas_call | solution.py:120
  43.5 2.0 copy-done
  45.6 2.2 copy-done.1
  47.8 20.7 %lookup.3 = bf16[64,32,256]{2,1,0:T(8,128)(2,1)S(1)} custom-call(s32[64,256]{1,0:T(8,128)S(1)} %get-tuple-element.29.row_ref, s32[64,256]{1,0:T(8,128)S(1)} %get-tuple-element.28.slot_ref, f32[7936,1,128]{2,1,0:T(1,128)S(1)} %copy-done.1), custom_call_target="tpu_custom_call" | custom-call | bytes 31457280 | tf_op jit(solution)/shard_map/lookup/pallas_call | solution.py:140
  68.8 43.8 %all_to_all.31 = bf16[512,4,256]{2,1,0:T(4,128)(2,1)S(1)} all-to-all(bf16[512,4,256]{2,1,0:T(4,128)(2,1)S(1)} %reshape.136), channel_id=1, replica_groups=mesh['dp'=64,'tensor'=8] {'dp','tensor'}, dimensions={0} | all-to-all | bytes 2097152 | tf_op jit(solution)/shard_map/embed_exchange/all_to_all | solution.py:286
  114.4 4.3 %all-to-all-start.2 = ((bf16[8,256,256]{2,1,0:T(8,128)(2,1)}), bf16[8,256,256]{2,1,0:T(8,128)(2,1)S(1)}, u32[]{:S(2)}, u32[]{:S(2)}) async-start(bf16[8,256,256]{2,1,0:T(8,128)(2,1)} %broadcast_in_dim.61), calls=%async_computation.2 | async-start | bytes 2097152 | tf_op jit(solution)/shard_map/embed_exchange/all_to_all | solution.py:23
  119.8 28.1 %all-to-all-done.2.x_ref = bf16[8,256,256]{2,1,0:T(8,128)(2,1)S(1)} async-done(((bf16[8,256,256]{2,1,0:T(8,128)(2,1)}), bf16[8,256,256]{2,1,0:T(8,128)(2,1)S(1)}, u32[]{:S(2)}, u32[]{:S(2)}) %all-to-all-start.2) | async-done | bytes 1048608 | tf_op jit(solution)/shard_map/embed_exchange/all_to_all | solution.py:23
  147.9 2.3 copy-done.2
  150.2 3.8 %forward.1 = (bf16[2048,256]{1,0:T(8,128)(2,1)S(1)}, f32[256,384]{1,0:T(8,128)S(1)}, f32[8,4,2048]{2,1,0:T(4,128)S(1)}, f32[4,2048]{1,0:T(4,128)S(1)}) custom-call(bf16[8,256,256]{2,1,0:T(8,128)(2,1)S(1)} %all-to-all-done.2.x_ref, f32[2048,1]{1,0:T(8,128)S(1)} %copy.11.gain_ref, bf16[16,256]{1,0:T(8,128)(2,1)S(1)} %and_convert_fusion.mask_ref, ...), custom_call_target="tpu_custom_call" | custom-call | flops 1207959552 | bytes 10485760 | tf_op jit(solution)/shard_map/forward/pallas_call | solution.py:229
  155.4 3.4 %all-to-all-start.3 = ((f32[8,4,2048]{2,1,0:T(4,128)}), f32[8,4,2048]{2,1,0:T(4,128)S(1)}, u32[]{:S(2)}, u32[]{:S(2)}) async-start(f32[8,4,2048]{2,1,0:T(4,128)} %copy-done.4), calls=%async_computation.3 | async-start | bytes 524288 | tf_op jit(solution)/shard_map/pool/all_to_all | solution.py:305
  158.8 12.0 %all-to-all-done.3 = f32[8,4,2048]{2,1,0:T(4,128)S(1)} async-done(((f32[8,4,2048]{2,1,0:T(4,128)}), f32[8,4,2048]{2,1,0:T(4,128)S(1)}, u32[]{:S(2)}, u32[]{:S(2)}) %all-to-all-start.3) | async-done | bytes 262176 | tf_op jit(solution)/shard_map/pool/all_to_all | solution.py:305
  173.6 5.4 %all-to-all-start.4 = ((bf16[64,4,1024]{2,1,0:T(4,128)(2,1)}), bf16[64,4,1024]{2,1,0:T(4,128)(2,1)S(1)}, u32[]{:S(2)}, u32[]{:S(2)}) async-start(bf16[64,4,1024]{2,1,0:T(4,128)(2,1)} %bitcast.4), calls=%async_computation.4 | async-start | bytes 1048576 | tf_op jit(solution)/shard_map/scores/all_to_all | solution.py:314
  180.2 16.2 %all-to-all-done.4 = bf16[64,4,1024]{2,1,0:T(4,128)(2,1)S(1)} async-done(((bf16[64,4,1024]{2,1,0:T(4,128)(2,1)}), bf16[64,4,1024]{2,1,0:T(4,128)(2,1)S(1)}, u32[]{:S(2)}, u32[]{:S(2)}) %all-to-all-start.4) | async-done | bytes 524320 | tf_op jit(solution)/shard_map/scores/all_to_all | solution.py:314
  196.4 2.4 collective-permute-start
  203.1 1.8 fusion
  205.5 2.1 collective-permute-start.1
  207.6 2.1 collective-permute-done.1
  209.6 1.3 add_convert_fusion
  211.0 5.5 %all-to-all-start.5 = ((bf16[32,32,384]{2,1,0:T(8,128)(2,1)}), bf16[32,32,384]{2,1,0:T(8,128)(2,1)S(1)}, u32[]{:S(2)}, u32[]{:S(2)}) async-start(bf16[32,32,384]{2,1,0:T(8,128)(2,1)} %bitcast.9), calls=%async_computation.5 | async-start | bytes 1572864 | tf_op jit(solution)/shard_map/backward/all_to_all | solution.py:357
  217.2 18.9 %all-to-all-done.5 = bf16[32,32,384]{2,1,0:T(8,128)(2,1)S(1)} async-done(((bf16[32,32,384]{2,1,0:T(8,128)(2,1)}), bf16[32,32,384]{2,1,0:T(8,128)(2,1)S(1)}, u32[]{:S(2)}, u32[]{:S(2)}) %all-to-all-start.5) | async-done | bytes 786464 | tf_op jit(solution)/shard_map/backward/all_to_all | solution.py:357
  (75 shorter events, 14.0 us)
Async XLA Ops:
  7.2 140.7 %all-gather.2.cloned.1.call-start = ((), (), s32[]{:S(2)}) async-start(), calls=%async_computation.6 | async-start | bytes 4792320 | tf_op jit(solution)/shard_map/weights/all_gather | solution.py:277
  33.8 11.7 %copy-start.6 = (s32[64,3,128]{2,1,0:T(4,128)}, s32[64,3,128]{2,1,0:T(4,128)S(1)}, u32[]{:S(2)}) copy-start(s32[64,3,128]{2,1,0:T(4,128)S(1)} %all_to_all.30) | copy-start | bytes 294916
  35.3 1.6 copy-start.3
  43.5 2.0 copy-start
  45.6 2.2 copy-start.1
  113.3 5.4 %copy-start.11 = (s32[2,2]{1,0:T(2,128)S(1)}, s32[2,2]{1,0:T(2,128)}, u32[]{:S(2)}) copy-start(s32[2,2]{1,0:T(2,128)} %param.9) | copy-start | bytes 52
  113.3 5.4 %copy-start.10 = (f32[2048]{0:T(1024)S(1)}, f32[2048]{0:T(1024)}, u32[]{:S(2)}) copy-start(f32[2048]{0:T(1024)} %param.12) | copy-start | bytes 24580
  114.4 33.5 %all-to-all-start.2 = ((bf16[8,256,256]{2,1,0:T(8,128)(2,1)}), bf16[8,256,256]{2,1,0:T(8,128)(2,1)S(1)}, u32[]{:S(2)}, u32[]{:S(2)}) async-start(bf16[8,256,256]{2,1,0:T(8,128)(2,1)} %broadcast_in_dim.61), calls=%async_computation.2 | async-start | bytes 2097152 | tf_op jit(solution)/shard_map/embed_exchange/all_to_all | solution.py:23
  147.9 2.3 copy-start.2
  154.0 0.7 copy-start.4
  154.8 0.6 copy-start.5
  155.4 15.4 %all-to-all-start.3 = ((f32[8,4,2048]{2,1,0:T(4,128)}), f32[8,4,2048]{2,1,0:T(4,128)S(1)}, u32[]{:S(2)}, u32[]{:S(2)}) async-start(f32[8,4,2048]{2,1,0:T(4,128)} %copy-done.4), calls=%async_computation.3 | async-start | bytes 524288 | tf_op jit(solution)/shard_map/pool/all_to_all | solution.py:305
  171.8 0.6 copy-start.7
  173.6 22.8 %all-to-all-start.4 = ((bf16[64,4,1024]{2,1,0:T(4,128)(2,1)}), bf16[64,4,1024]{2,1,0:T(4,128)(2,1)S(1)}, u32[]{:S(2)}, u32[]{:S(2)}) async-start(bf16[64,4,1024]{2,1,0:T(4,128)(2,1)} %bitcast.4), calls=%async_computation.4 | async-start | bytes 1048576 | tf_op jit(solution)/shard_map/scores/all_to_all | solution.py:314
  196.4 3.9 %collective-permute-start = (bf16[64,4,1024]{2,1,0:T(4,128)(2,1)S(1)}, bf16[64,4,1024]{2,1,0:T(4,128)(2,1)S(1)}, u32[]{:S(2)}, u32[]{:S(2)}) collective-permute-start(bf16[64,4,1024]{2,1,0:T(4,128)(2,1)S(1)} %all-to-all-done.4), channel_id=1, source_target_pairs={{0,8},{8,0},{16,24},{24,16},{32,40},{40,32},{48,56},{56,48},{64,72... | collective-permute-start | bytes 1572872 | tf_op jit(solution)/shard_map/scores/ppermute | solution.py:317
  200.3 0.8 copy-start.9
  200.7 2.3 copy-start.8
  200.7 2.4 copy-start.12
  205.5 4.2 %collective-permute-start.1 = (bf16[1024,384]{1,0:T(8,128)(2,1)S(1)}, bf16[1024,384]{1,0:T(8,128)(2,1)S(1)}, u32[]{:S(2)}, u32[]{:S(2)}) collective-permute-start(bf16[1024,384]{1,0:T(8,128)(2,1)S(1)} %convolution_convert_fusion), channel_id=1, source_target_pairs={{0,8},{8,0},{16,24},{24,16},{32,40},{40,32},{48,56},{56,48},{64,72... | collective-permute-start | bytes 2359304 | tf_op jit(solution)/shard_map/backward/ppermute | solution.py:354
  211.0 25.1 %all-to-all-start.5 = ((bf16[32,32,384]{2,1,0:T(8,128)(2,1)}), bf16[32,32,384]{2,1,0:T(8,128)(2,1)S(1)}, u32[]{:S(2)}, u32[]{:S(2)}) async-start(bf16[32,32,384]{2,1,0:T(8,128)(2,1)} %bitcast.9), calls=%async_computation.5 | async-start | bytes 1572864 | tf_op jit(solution)/shard_map/backward/all_to_all | solution.py:357
Sparse Core Ops, SparseCore 0:
  35.4 94.7 all-gather.1
